TPU v7x, 128 devices: a whole 4x4x4 slice. The times are simulated.
128 devices in a mesh: dp: 16 (over z_lo, y, core), seq: 8 (over x, z_hi).
Axes of the slice: x: 4, y: 4, z: 4 (z_hi: 2, z_lo: 2; z = z_hi * 2 + z_lo), core: 2. Of those that a mesh axis runs over, the one named last changes fastest.
Arguments:
- tokens: bfloat16 [16, 16, 256, 1152], P('dp', 'seq'), may hold values from -6 to 6
- mod_shift: float32 [16, 1152], P('dp'), may hold values from -3 to 3
- mod_scale: float32 [16, 1152], P('dp'), may hold values from -2.5 to 2.5
- res_gate: float32 [16, 1152], P('dp'), may hold values from -4 to 4
- qkv_weight: bfloat16 [1152, 3456], replicated, may hold values from -0.1875 to 0.1875
- out_weight: bfloat16 [1152, 1152], replicated, may hold values from -0.1875 to 0.1875
- query_gain: float32 [72], replicated, may hold values from 0.1 to 1.9
- key_gain: float32 [72], replicated, may hold values from 0.1 to 1.9
- cotangent: bfloat16 [16, 16, 256, 1152], P('dp', 'seq'), may hold values from -6 to 6
Outputs:
- block_output: bfloat16 [16, 16, 256, 1152], P('dp', 'seq')
- grad_tokens: bfloat16 [16, 16, 256, 1152], P('dp', 'seq')
- grad_qkv_weight: bfloat16 [1152, 3456], P(('dp', 'seq'))
- grad_out_weight: bfloat16 [1152, 1152], P(('dp', 'seq'))
All inputs are finite; a program needn't handle non-finite values.
Results may differ from a plain program's by a relative error of at most 0.019.
Values may be sent and summed in bfloat16 or wider, within the bound.
A program may use at most 192 MiB of HBM per device.

v0:
```python
import jax
import jax.numpy as jnp
from jax import lax
from jax.sharding import PartitionSpec as P


def modulate(tokens_f32, mod_shift, mod_scale):
    row_mean = jnp.mean(tokens_f32, axis=-1, keepdims=True)
    centered = tokens_f32 - row_mean
    variance = jnp.mean(centered * centered, axis=-1, keepdims=True)
    normed = centered * lax.rsqrt(variance + 1e-06)
    return normed * (1.0 + mod_scale[:, None, None, :]) + mod_shift[:, None, None, :]


def rms_gain(inputs, gain_vector, factor):
    as_float = inputs.astype(jnp.float32)
    mean_square = jnp.mean(as_float * as_float, axis=-1, keepdims=True)
    return (as_float * lax.rsqrt(mean_square + 1e-06) * gain_vector * factor).astype(jnp.bfloat16)


def attend(queries, key_block, value_block, query_gain, key_gain):
    head_dim = query_gain.shape[0]
    num_heads = queries.shape[-1] // head_dim

    def split_heads(tensor):
        return tensor.reshape(tensor.shape[:3] + (num_heads, head_dim))

    query_norm = rms_gain(split_heads(queries), query_gain, head_dim ** (-0.5))
    key_norm = rms_gain(split_heads(key_block), key_gain, 1.0)
    scores = jnp.einsum(
        "vfphd,vgphd->vphfg", query_norm, key_norm, preferred_element_type=jnp.float32
    )
    weights = jnp.exp(scores)
    probabilities = (weights / jnp.sum(weights, axis=-1, keepdims=True)).astype(jnp.bfloat16)
    result = jnp.einsum(
        "vphfg,vgphd->vfphd",
        probabilities,
        split_heads(value_block),
        preferred_element_type=jnp.float32,
    )
    return result.reshape(queries.shape).astype(jnp.bfloat16)


def flat_dot(left_side, right_side):
    flattened = left_side.reshape(-1, left_side.shape[-1])
    product = jnp.dot(flattened, right_side, preferred_element_type=jnp.float32)
    return product.reshape(left_side.shape[:-1] + (right_side.shape[-1],))


def flat_dot_t(left_side, right_side):
    flattened = left_side.reshape(-1, left_side.shape[-1])
    product = lax.dot_general(
        flattened, right_side, (((1,), (1,)), ((), ())), preferred_element_type=jnp.float32
    )
    return product.reshape(left_side.shape[:-1] + (right_side.shape[0],))


def on_device(
    tokens, mod_shift, mod_scale, res_gate, qkv_weight, out_weight, query_gain, key_gain, cotangent
):
    width = tokens.shape[-1]
    tokens_f32 = tokens.astype(jnp.float32)
    modulated, pull_mod = jax.vjp(lambda tensor: modulate(tensor, mod_shift, mod_scale), tokens_f32)
    hidden = modulated.astype(jnp.bfloat16)
    projected_local = flat_dot(hidden, qkv_weight).astype(jnp.bfloat16)
    projected = lax.all_to_all(projected_local, "seq", split_axis=2, concat_axis=1, tiled=True)
    queries = projected[..., :width]
    key_block = projected[..., width : 2 * width]
    value_block = projected[..., 2 * width :]
    owned_attended, pull_att = jax.vjp(
        lambda first, second, third: attend(first, second, third, query_gain, key_gain),
        queries,
        key_block,
        value_block,
    )
    attended = lax.all_to_all(owned_attended, "seq", split_axis=1, concat_axis=2, tiled=True)
    projection = flat_dot(attended, out_weight)
    gate_bcast = res_gate[:, None, None, :]
    block_output = (tokens_f32 + gate_bcast * projection).astype(jnp.bfloat16)
    grad_projection = (cotangent.astype(jnp.float32) * gate_bcast).astype(jnp.bfloat16)
    grad_attended = flat_dot_t(grad_projection, out_weight).astype(jnp.bfloat16)
    grad_att_owned = lax.all_to_all(grad_attended, "seq", split_axis=2, concat_axis=1, tiled=True)
    grad_query, grad_keys, grad_values = pull_att(grad_att_owned)
    grad_proj_owned = jnp.concatenate([grad_query, grad_keys, grad_values], axis=-1)
    grad_proj_local = lax.all_to_all(
        grad_proj_owned, "seq", split_axis=1, concat_axis=2, tiled=True
    )
    grad_hidden = flat_dot_t(grad_proj_local, qkv_weight).astype(jnp.bfloat16)
    (grad_mod,) = pull_mod(grad_hidden.astype(jnp.float32))
    grad_tokens = (cotangent.astype(jnp.float32) + grad_mod).astype(jnp.bfloat16)
    left_flat = hidden.reshape(-1, width)
    right_flat = grad_proj_local.reshape(-1, 3 * width)
    attended_flat = attended.reshape(-1, width)
    grad_proj_flat = grad_projection.reshape(-1, width)
    part_projected = lax.dot_general(
        left_flat, right_flat, (((0,), (0,)), ((), ())), preferred_element_type=jnp.float32
    )
    part_output = lax.dot_general(
        attended_flat, grad_proj_flat, (((0,), (0,)), ((), ())), preferred_element_type=jnp.float32
    )
    summed = lax.psum_scatter(
        jnp.concatenate([part_projected, part_output], axis=1),
        ("dp", "seq"),
        scatter_dimension=0,
        tiled=True,
    )
    grad_qkv_weight = summed[:, : 3 * width].astype(jnp.bfloat16)
    grad_out_weight = summed[:, 3 * width :].astype(jnp.bfloat16)
    return (block_output, grad_tokens, grad_qkv_weight, grad_out_weight)


def solution(mesh):
    in_specs = (
        P("dp", "seq", None, None),
        P("dp", None),
        P("dp", None),
        P("dp", None),
        P(),
        P(),
        P(),
        P(),
        P("dp", "seq", None, None),
    )
    out_specs = (
        P("dp", "seq", None, None),
        P("dp", "seq", None, None),
        P(("dp", "seq"), None),
        P(("dp", "seq"), None),
    )
    return jax.shard_map(
        on_device, mesh=mesh, in_specs=in_specs, out_specs=out_specs, check_vma=False
    )
```

profile of v0, /device:TPU:0, one launch (start us, length us, event | category | flops | bytes accessed | tf_op | source)
XLA Modules:
  0.0 463.1 jit_solution(14041258269067135902)
XLA Ops:
  3.0 1.9 fusion.39
  4.9 2.2 copy.179
  7.2 7.7 %all-to-all-start.2 = ((bf16[1,2,256,1152]{3,1,0,2:T(2,128)(2,1)}), bf16[1,2,256,1152]{3,1,0,2:T(2,128)(2,1)}, u32[]{:S(2)}, u32[]{:S(2)}) async-start(bf16[1,2,256,1152]{3,1,0,2:T(2,128)(2,1)} %copy.179), calls=%async_computation.2 | async-start | bytes 2359296 | tf_op jit(solution)/shard_map/all_to_all | solution.py:82
  16.5 1.7 fusion.44
  19.8 8.4 %fusion.7 = bf16[1,2,256,3456]{3,2,1,0:T(8,128)(2,1)S(1)} fusion(bf16[1152,3456]{1,0:T(8,128)(2,1)} %param.13, bf16[1,2,256,1152]{3,2,1,0:T(8,128)(2,1)S(1)} %fusion.47), kind=kOutput, calls=%fused_computation.8 | convolution fusion | flops 4078632960 | bytes 12681216 | tf_op jit(solution)/shard_map/dot_general | solution.py:46
  28.2 5.4 %copy.165 = bf16[1,2,256,3456]{3,1,0,2:T(2,128)(2,1)} copy(bf16[1,2,256,3456]{3,2,1,0:T(8,128)(2,1)S(1)} %fusion.7) | data formatting | bytes 7077888 | tf_op jit(solution)/shard_map/convert_element_type | solution.py:65
  33.7 7.6 %all-to-all-start = ((bf16[1,2,256,3456]{3,1,0,2:T(2,128)(2,1)}), bf16[1,2,256,3456]{3,1,0,2:T(2,128)(2,1)}, u32[]{:S(2)}, u32[]{:S(2)}) async-start(bf16[1,2,256,3456]{3,1,0,2:T(2,128)(2,1)} %copy.165), calls=%async_computation | async-start | bytes 7077888 | tf_op jit(solution)/shard_map/all_to_all | solution.py:66
  41.4 2.4 copy.244
  43.8 5.7 %reshape.360 = bf16[1,16,32,16,72]{4,3,2,1,0:T(8,128)(2,1)} reshape(bf16[1,8,2,32,1152]{4,3,2,1,0:T(8,128)(2,1)} %bitcast.151) | data formatting | bytes 2359296 | tf_op jit(solution)/shard_map/transpose(jvp())/reshape | solution.py:41
  49.5 42.0 %all-to-all-done = bf16[1,2,256,3456]{3,1,0,2:T(2,128)(2,1)} async-done(((bf16[1,2,256,3456]{3,1,0,2:T(2,128)(2,1)}), bf16[1,2,256,3456]{3,1,0,2:T(2,128)(2,1)}, u32[]{:S(2)}, u32[]{:S(2)}) %all-to-all-start) | async-done | bytes 3538976 | tf_op jit(solution)/shard_map/all_to_all | solution.py:66
  91.5 2.4 copy.166
  94.3 2.8 slice_convert_fusion.1
  97.1 6.2 %reshape.371 = f32[16,32,16,72]{3,2,1,0:T(8,128)} reshape(f32[1,16,32,1152]{3,2,1,0:T(8,128)} %get-tuple-element.5) | data formatting | bytes 4718592 | tf_op jit(solution)/shard_map/jvp()/convert_element_type | solution.py:16
  103.3 6.2 %reshape.372 = f32[1,16,32,16,72]{4,3,2,1,0:T(8,128)} reshape(f32[1,16,32,1152]{3,2,1,0:T(8,128)} %get-tuple-element.5) | data formatting | bytes 4718592 | tf_op jit(solution)/shard_map/jvp()/convert_element_type | solution.py:16
  109.4 6.2 %reshape.369 = f32[16,32,16,72]{3,2,1,0:T(8,128)} reshape(f32[1,16,32,1152]{3,2,1,0:T(8,128)} %get-tuple-element.4) | data formatting | bytes 4718592 | tf_op jit(solution)/shard_map/jvp()/convert_element_type | solution.py:16
  115.6 6.2 %reshape.370 = f32[1,16,32,16,72]{4,3,2,1,0:T(8,128)} reshape(f32[1,16,32,1152]{3,2,1,0:T(8,128)} %get-tuple-element.4) | data formatting | bytes 4718592 | tf_op jit(solution)/shard_map/jvp()/convert_element_type | solution.py:16
  121.8 3.4 multiply_reduce_fusion
  127.0 3.4 multiply_reduce_fusion.1
  131.6 5.7 %reshape.359 = bf16[16,32,16,72]{3,2,1,0:T(8,128)(2,1)} reshape(bf16[1,16,32,1152]{3,2,1,0:T(8,128)(2,1)} %get-tuple-element.6) | data formatting | bytes 2359296 | tf_op jit(solution)/shard_map/reshape.13
  137.3 5.2 %multiply_convert_fusion = (bf16[16,32,16,72]{3,2,1,0:T(8,128)(2,1)S(1)}, bf16[16,32,16,72]{3,2,1,0:T(8,128)(2,1)S(1)}) fusion(f32[16,32,16,72]{3,2,1,0:T(8,128)} %reshape.371, f32[72]{0:T(128)S(1)} %copy-done.24, f32[16,32,16]{2,1,0:T(8,128)} %copy.171, f32[72]{0:T(128)S(1)} %copy-done.25, f32[16,32,16,72]{3,2,1,0:T(8,128)} %reshape.369, ...), kind=kLoop, calls=%fused_computation.28 | loop fusion | flops 4128768 | bytes 7144000 | tf_op jit(solution)/shard_map/jvp()/convert_element_type | solution.py:18
  142.6 3.1 exponential_reduce_fusion
  146.6 1.9 convert_bitcast_fusion.1
  148.5 1.9 copy.176
  150.4 4.6 convert_element_type.211
  155.0 12.8 %all-to-all-start.1 = ((bf16[1,16,32,1152]{3,2,0,1:T(8,128)(2,1)}), bf16[1,16,32,1152]{3,2,0,1:T(8,128)(2,1)}, u32[]{:S(2)}, u32[]{:S(2)}) async-start(bf16[1,16,32,1152]{3,2,0,1:T(8,128)(2,1)} %bitcast.150), calls=%async_computation.1 | async-start | bytes 2359296 | tf_op jit(solution)/shard_map/all_to_all | solution.py:76
  167.8 4.5 convert_bitcast_fusion
  172.3 1.9 copy.198
  174.2 4.6 reshape.364
  178.8 7.0 %fusion.13 = (f32[32,16,16]{2,1,0:T(8,128)S(1)}, bf16[32,16,16,16]{2,3,1,0:T(8,128)(2,1)S(1)}) fusion(f32[32,16,16,16]{2,3,1,0:T(8,128)} %copy-done.5, f32[32,16,16]{2,1,0:T(8,128)} %multiply_divide_fusion, bf16[16,32,16,72]{3,2,1,0:T(8,128)(2,1)} %reshape.359, bf16[1,16,32,16,72]{4,3,2,1,0:T(8,128)(2,1)} %reshape.360), kind=kOutput, calls=%fused_computation.14 | convolution fusion | flops 19521536 | bytes 3211264 | tf_op jit(solution)/shard_map/transpose(jvp(vphfg,vgphd->vfphd))/dot_general | solution.py:35
  185.9 5.9 %fusion.19 = (f32[16,32,16]{0,2,1:T(8,128)}, bf16[32,16,16,72]{3,2,1,0:T(8,128)(2,1)}) fusion(f32[1,16,32,16,72]{4,3,2,1,0:T(8,128)S(1)} %copy-done.1, f32[72]{0:T(128)S(1)} %copy-done.24, bf16[16,32,16,72]{3,2,1,0:T(8,128)(2,1)S(1)} %copy-done.10, bf16[32,16,16,16]{2,3,1,0:T(8,128)(2,1)S(1)} %get-tuple-element.10, f32[32,16,16,16]{2,3,1,0:T(8,128)S(1)} %copy-done.6, ...), kind=kOutput, calls=%fused_computation.21 | convolution fusion | flops 22339584 | bytes 5603616 | tf_op jit(solution)/shard_map/transpose(jvp(vfphd,vgphd->vphfg))/dot_general | solution.py:30
  193.1 5.6 %fusion.15 = bf16[1,16,32,16,72]{4,1,3,2,0:T(8,128)(2,1)S(1)} fusion(f32[1,16,32,16,72]{4,3,2,1,0:T(8,128)} %reshape.372, bf16[32,16,16,72]{3,2,1,0:T(8,128)(2,1)} %get-tuple-element.12, f32[16,32,16]{0,2,1:T(8,128)S(1)} %copy.195, f32[16,32,16]{0,2,1:T(8,128)} %copy.192, f32[72]{0:T(128)S(1)} %copy-done.24), kind=kLoop, calls=%fused_computation.16 | loop fusion | flops 4128768 | bytes 4784416 | tf_op jit(solution)/shard_map/transpose(jvp())/convert_element_type | solution.py:16
  198.7 1.9 copy.197
  200.6 4.8 %reshape.363 = bf16[1,16,32,1152]{3,2,1,0:T(8,128)(2,1)} reshape(bf16[1,16,32,16,72]{4,3,2,1,0:T(8,128)(2,1)} %copy.197) | data formatting | bytes 2359296 | tf_op jit(solution)/shard_map/transpose(jvp())/reshape | solution.py:26
  205.4 11.5 %fusion.23 = (f32[16,32,16]{0,2,1:T(8,128)}, bf16[32,16,16,72]{3,2,1,0:T(8,128)(2,1)}) fusion(f32[1,16,32,16,72]{4,3,2,1,0:T(8,128)} %reshape.370, f32[72]{0:T(128)S(1)} %broadcast_multiply_fusion.1, bf16[16,32,16,72]{3,2,1,0:T(8,128)(2,1)} %copy-done.8, bf16[32,16,16,16]{2,3,1,0:T(8,128)(2,1)} %copy-done.15, f32[32,16,16,16]{2,3,1,0:T(8,128)} %copy-done.5, ...), kind=kOutput, calls=%fused_computation.26 | convolution fusion | flops 22339584 | bytes 5603616 | tf_op jit(solution)/shard_map/transpose(jvp(vfphd,vgphd->vphfg))/dot_general | solution.py:30
  218.3 5.5 %fusion.14 = bf16[1,16,32,16,72]{4,1,3,2,0:T(8,128)(2,1)S(1)} fusion(f32[1,16,32,16,72]{4,3,2,1,0:T(8,128)} %reshape.370, bf16[32,16,16,72]{3,2,1,0:T(8,128)(2,1)} %get-tuple-element.14, f32[16,32,16]{0,2,1:T(8,128)S(1)} %copy.188, f32[16,32,16]{0,2,1:T(8,128)S(1)} %copy.185, f32[72]{0:T(128)S(1)} %broadcast_multiply_fusion.1), kind=kLoop, calls=%fused_computation.15 | loop fusion | flops 4128768 | bytes 4784416 | tf_op jit(solution)/shard_map/transpose(jvp())/convert_element_type | solution.py:16
  223.9 1.9 copy.190
  225.8 4.6 reshape.362
  230.4 3.4 maximum_bitcast_fusion
  233.7 7.2 %all-to-all-start.3 = ((bf16[1,16,32,3456]{3,2,0,1:T(8,128)(2,1)}), bf16[1,16,32,3456]{3,2,0,1:T(8,128)(2,1)}, u32[]{:S(2)}, u32[]{:S(2)}) async-start(bf16[1,16,32,3456]{3,2,0,1:T(8,128)(2,1)} %maximum_bitcast_fusion), calls=%async_computation.3 | async-start | bytes 7077888 | tf_op jit(solution)/shard_map/all_to_all | solution.py:85
  242.6 4.1 fusion.76
  246.7 2.9 fusion.29
  249.6 40.6 %all-to-all-done.3 = bf16[1,16,32,3456]{3,2,0,1:T(8,128)(2,1)} async-done(((bf16[1,16,32,3456]{3,2,0,1:T(8,128)(2,1)}), bf16[1,16,32,3456]{3,2,0,1:T(8,128)(2,1)}, u32[]{:S(2)}, u32[]{:S(2)}) %all-to-all-start.3) | async-done | bytes 3538976 | tf_op jit(solution)/shard_map/all_to_all | solution.py:85
  290.2 2.4 copy.200
  292.6 4.5 fusion.75
  297.2 7.6 %pad_maximum_fusion = f32[1152,4608]{1,0:T(8,128)} fusion(f32[1152,1152]{1,0:T(8,128)S(1)} %bitcast.145, f32[1152,3456]{1,0:T(8,128)S(1)} %fusion.75), kind=kLoop, calls=%fused_computation | loop fusion | flops 5308416 | bytes 42467328 | tf_op jit(solution)/shard_map/concatenate | solution.py:102
  304.8 142.8 %all-reduce.2 = bf16[1152,4608]{1,0:T(8,128)(2,1)} all-reduce(f32[1152,4608]{1,0:T(8,128)} %pad_maximum_fusion), channel_id=2, replica_groups=mesh['dp'=16,'seq'=8] {'dp','seq'}, use_global_device_ids=true, to_apply=%region_10.0.clone | all-reduce | flops 5308416 | bytes 31850496
  449.9 9.6 %fusion.48 = (f32[2,256]{1,0:T(2,128)S(1)}, f32[2,256,1152]{2,1,0:T(8,128)S(1)}) fusion(bf16[1,2,256,1152]{3,2,1,0:T(8,128)(2,1)} %param.9, f32[2,256]{1,0:T(2,128)S(1)} %broadcast_multiply_fusion, f32[1152]{0:T(1024)S(1)} %add_reduce_fusion, bf16[2,256,3456]{2,1,0:T(8,128)(2,1)} %bitcast.154, bf16[1152,3456]{1,0:T(8,128)(2,1)} %param.13), kind=kOutput, calls=%fused_computation.60 | convolution fusion | flops 4080991744 | bytes 15049216 | tf_op jit(solution)/shard_map/dot_general | solution.py:52
  460.8 1.9 fusion.43
  (92 shorter events, 17.7 us)
Async XLA Ops:
  0.6 2.4 copy-start
  3.0 1.9 copy-start.12
  4.9 9.9 %copy-start.23 = (f32[1,1152]{1,0:T(1,128)S(1)}, f32[1,1152]{1,0:T(1,128)}, u32[]{:S(2)}) copy-start(f32[1,1152]{1,0:T(1,128)} %param.10) | copy-start | bytes 13828
  4.9 10.0 %copy-start.22 = (f32[1,1152]{1,0:T(1,128)S(1)}, f32[1,1152]{1,0:T(1,128)}, u32[]{:S(2)}) copy-start(f32[1,1152]{1,0:T(1,128)} %param.11) | copy-start | bytes 13828
  7.2 26.5 %all-to-all-start.2 = ((bf16[1,2,256,1152]{3,1,0,2:T(2,128)(2,1)}), bf16[1,2,256,1152]{3,1,0,2:T(2,128)(2,1)}, u32[]{:S(2)}, u32[]{:S(2)}) async-start(bf16[1,2,256,1152]{3,1,0,2:T(2,128)(2,1)} %copy.179), calls=%async_computation.2 | async-start | bytes 2359296 | tf_op jit(solution)/shard_map/all_to_all | solution.py:82
  14.9 3.4 copy-start.2
  18.8 1.0 copy-start.16
  33.7 7.7 %copy-start.25 = (f32[72]{0:T(128)S(1)}, f32[72]{0:T(128)}, u32[]{:S(2)}) copy-start(f32[72]{0:T(128)} %param.15) | copy-start | bytes 868
  33.7 57.9 %all-to-all-start = ((bf16[1,2,256,3456]{3,1,0,2:T(2,128)(2,1)}), bf16[1,2,256,3456]{3,1,0,2:T(2,128)(2,1)}, u32[]{:S(2)}, u32[]{:S(2)}) async-start(bf16[1,2,256,3456]{3,1,0,2:T(2,128)(2,1)} %copy.165), calls=%async_computation | async-start | bytes 7077888 | tf_op jit(solution)/shard_map/all_to_all | solution.py:66
  130.4 6.9 %copy-start.24 = (f32[72]{0:T(128)S(1)}, f32[72]{0:T(128)}, u32[]{:S(2)}) copy-start(f32[72]{0:T(128)} %param.16) | copy-start | bytes 868
  142.5 3.2 copy-start.8
  142.5 3.2 copy-start.9
  142.5 4.0 copy-start.7
  145.7 2.8 copy-start.5
  145.7 2.8 copy-start.18
  155.0 78.8 %all-to-all-start.1 = ((bf16[1,16,32,1152]{3,2,0,1:T(8,128)(2,1)}), bf16[1,16,32,1152]{3,2,0,1:T(8,128)(2,1)}, u32[]{:S(2)}, u32[]{:S(2)}) async-start(bf16[1,16,32,1152]{3,2,0,1:T(8,128)(2,1)} %bitcast.150), calls=%async_computation.1 | async-start | bytes 2359296 | tf_op jit(solution)/shard_map/all_to_all | solution.py:76
  178.8 7.1 %copy-start.1 = (f32[1,16,32,16,72]{4,3,2,1,0:T(8,128)S(1)}, f32[1,16,32,16,72]{4,3,2,1,0:T(8,128)}, u32[]{:S(2)}) copy-start(f32[1,16,32,16,72]{4,3,2,1,0:T(8,128)} %reshape.372) | copy-start | bytes 7077892
  178.8 7.1 %copy-start.6 = (f32[32,16,16,16]{2,3,1,0:T(8,128)S(1)}, f32[32,16,16,16]{2,3,1,0:T(8,128)}, u32[]{:S(2)}) copy-start(f32[32,16,16,16]{2,3,1,0:T(8,128)} %copy-done.5) | copy-start | bytes 1572868
  178.8 7.1 %copy-start.10 = (bf16[16,32,16,72]{3,2,1,0:T(8,128)(2,1)S(1)}, bf16[16,32,16,72]{3,2,1,0:T(8,128)(2,1)}, u32[]{:S(2)}) copy-start(bf16[16,32,16,72]{3,2,1,0:T(8,128)(2,1)} %copy-done.9) | copy-start | bytes 3538948
  178.8 7.1 %copy-start.19 = (f32[32,16,16]{2,1,0:T(8,128)S(1)}, f32[32,16,16]{2,1,0:T(8,128)}, u32[]{:S(2)}) copy-start(f32[32,16,16]{2,1,0:T(8,128)} %copy-done.18) | copy-start | bytes 98308
  185.8 6.0 %copy-start.15 = (bf16[32,16,16,16]{2,3,1,0:T(8,128)(2,1)}, bf16[32,16,16,16]{2,3,1,0:T(8,128)(2,1)S(1)}, u32[]{:S(2)}) copy-start(bf16[32,16,16,16]{2,3,1,0:T(8,128)(2,1)S(1)} %get-tuple-element.10) | copy-start | bytes 786436
  185.8 5.9 %copy-start.21 = (f32[32,16,16]{2,1,0:T(8,128)}, f32[32,16,16]{2,1,0:T(8,128)S(1)}, u32[]{:S(2)}) copy-start(f32[32,16,16]{2,1,0:T(8,128)S(1)} %neg.10) | copy-start | bytes 98308
  200.6 4.8 %copy-start.20 = (f32[32,16,16]{2,1,0:T(8,128)S(1)}, f32[32,16,16]{2,1,0:T(8,128)}, u32[]{:S(2)}) copy-start(f32[32,16,16]{2,1,0:T(8,128)} %copy-done.18) | copy-start | bytes 98308
  233.7 56.4 %all-to-all-start.3 = ((bf16[1,16,32,3456]{3,2,0,1:T(8,128)(2,1)}), bf16[1,16,32,3456]{3,2,0,1:T(8,128)(2,1)}, u32[]{:S(2)}, u32[]{:S(2)}) async-start(bf16[1,16,32,3456]{3,2,0,1:T(8,128)(2,1)} %maximum_bitcast_fusion), calls=%async_computation.3 | async-start | bytes 7077888 | tf_op jit(solution)/shard_map/all_to_all | solution.py:85
  241.0 1.6 copy-start.13
  242.6 4.1 copy-start.3
  290.2 2.5 copy-start.17
  290.2 7.0 %slice-start = ((s8[5308416]{0:T(1024)(128)(4,1)}), s8[4194304]{0:T(1024)(128)(4,1)S(1)}, s32[]{:S(2)}) async-start(s8[5308416]{0:T(1024)(128)(4,1)} %bitcast.144), calls=%async_computation.4 | async-start | bytes 8388608
  292.6 4.5 copy-start.14
  292.6 4.5 slice-start.1
  449.9 9.7 %copy-start.4 = (bf16[1,2,256,1152]{3,2,1,0:T(8,128)(2,1)S(1)}, bf16[1,2,256,1152]{3,2,1,0:T(8,128)(2,1)}, u32[]{:S(2)}) copy-start(bf16[1,2,256,1152]{3,2,1,0:T(8,128)(2,1)} %param.9) | copy-start | bytes 3538948
  459.5 1.3 copy-start.11
where the time goes:
time: 472 us; the launch traced here: 463 us
  blocking collectives  143 us (30%)
  local copies, waits for them, and re-layouts  88.4 us (19%)
  waiting for transfers between devices  82.6 us (18%)
  matrix products  65.4 us (14%)
  other arithmetic  46.7 us (10%)
  starting transfers between devices  35.4 us (8%)
    unnamed x1, blocking collectives  143 us
    all_to_all x1, waiting for transfers between devices, on_device(): lax.all_to_all(projected_local, 'seq', split_axis=2, concat_axis=1, tiled...  42 us
    all_to_all x1, waiting for transfers between devices, on_device(): lax.all_to_all(grad_proj_owned, 'seq', split_axis=1, concat_axis=2, tiled...  40.6 us
    convert_element_type x6, local copies, waits for them, and re-layouts, rms_gain(): as_float = inputs.astype(jnp.float32)  28.4 us
    dot_general x3, matrix products, attend(): jnp.einsum('vfphd,vgphd->vphfg', query_norm, key_norm, preferred_element_...  20.6 us
    reshape x3, local copies, waits for them, and re-layouts, split_heads(): return tensor.reshape(tensor.shape[:3] + (num_heads, head_dim))  14 us
    convert_element_type x3, other arithmetic, rms_gain(): as_float = inputs.astype(jnp.float32)  14 us
    dot_general x3, matrix products, attend(): jnp.einsum('vphfg,vgphd->vfphd', probabilities, split_heads(value_block),...  13.4 us
  transfers between devices with their start and end apart: 4, of which 2 were waited for; matrix products, arithmetic and copies ran while one was open for 22% of the time, Pallas kernels for 0%

commit v1 on v0

v1 whole, which is shorter than its diff:
```python
import jax
import jax.numpy as jnp
from jax import lax
from jax.experimental import pallas as pl
from jax.experimental.pallas import tpu as pltpu
from jax.sharding import PartitionSpec as P

F32 = jnp.float32
BF16 = jnp.bfloat16
D = 1152
HD = 72
NH = 16


def dot_nn(a, b):
    return lax.dot_general(a, b, (((1,), (0,)), ((), ())), preferred_element_type=F32)


def dot_nt(a, b):
    return lax.dot_general(a, b, (((1,), (1,)), ((), ())), preferred_element_type=F32)


def dot_tn(a, b):
    return lax.dot_general(a, b, (((0,), (0,)), ((), ())), preferred_element_type=F32)


def ln_stats(x):
    mean = jnp.mean(x, axis=-1, keepdims=True)
    xc = x - mean
    var = jnp.mean(xc * xc, axis=-1, keepdims=True)
    return xc, lax.rsqrt(var + 1e-6)


CH = 32


def compute_kernel(tok, cot, shift, scale, gate, wqkv, wo, qg, kg, out, gtok, gw,
                   hid, proj, gp, gatt, att, dproj, hidt):
    n = tok.shape[0]
    groups = n // 256

    def phase_a(i, c):
        r = pl.ds(pl.multiple_of(i * CH, CH), CH)
        x = tok[r, :].astype(F32)
        xc, rs = ln_stats(x)
        hid[r, :] = (xc * rs * (1.0 + scale[...]) + shift[...]).astype(BF16)
        gp[r, :] = (cot[r, :].astype(F32) * gate[...]).astype(BF16)
        return c

    lax.fori_loop(0, n // CH, phase_a, 0)
    for b in range(3):
        cs = pl.ds(b * D, D)
        proj[:, cs] = dot_nn(hid[...], wqkv[:, cs]).astype(BF16)
    gatt[...] = dot_nt(gp[...], wo[...]).astype(BF16)

    ri = lax.broadcasted_iota(jnp.int32, (256, 256), 0)
    ci = lax.broadcasted_iota(jnp.int32, (256, 256), 1)
    mask = jnp.where((ri & 15) == (ci & 15), 1.0, 0.0).astype(F32)
    qgain = qg[...] * (HD ** -0.5)
    kgain = kg[...]

    def phase_c(g, c):
        r = pl.ds(pl.multiple_of(g * 256, 256), 256)
        for h in range(NH):
            q = proj[r, pl.ds(h * HD, HD)].astype(F32)
            k = proj[r, pl.ds(D + h * HD, HD)].astype(F32)
            v = proj[r, pl.ds(2 * D + h * HD, HD)]
            da = gatt[r, pl.ds(h * HD, HD)]
            rq = lax.rsqrt(jnp.mean(q * q, axis=-1, keepdims=True) + 1e-6)
            rk = lax.rsqrt(jnp.mean(k * k, axis=-1, keepdims=True) + 1e-6)
            qh = q * rq
            kh = k * rk
            qn = (qh * qgain).astype(BF16)
            kn = (kh * kgain).astype(BF16)
            s = dot_nt(qn, kn)
            e = jnp.exp(s) * mask
            p = e * (1.0 / jnp.sum(e, axis=-1, keepdims=True))
            pb = p.astype(BF16)
            a = dot_nn(pb, v)
            ab = a.astype(BF16)
            att[r, pl.ds(h * HD, HD)] = ab
            dp = dot_nt(da, v)
            delta = jnp.sum(da.astype(F32) * a, axis=-1, keepdims=True)
            ds = (p * (dp - delta)).astype(BF16)
            dv = dot_tn(pb, da)
            dqn = dot_nn(ds, kn) * qgain
            dkn = dot_tn(ds, qn) * kgain
            dq = rq * (dqn - qh * jnp.mean(dqn * qh, axis=-1, keepdims=True))
            dk = rk * (dkn - kh * jnp.mean(dkn * kh, axis=-1, keepdims=True))
            dproj[r, pl.ds(h * HD, HD)] = dq.astype(BF16)
            dproj[r, pl.ds(D + h * HD, HD)] = dk.astype(BF16)
            dproj[r, pl.ds(2 * D + h * HD, HD)] = dv.astype(BF16)
        return c

    lax.fori_loop(0, groups, phase_c, 0)

    po = dot_nn(att[...], wo[...])
    out[...] = (tok[...].astype(F32) + gate[...] * po).astype(BF16)

    hidt[...] = att[...].T
    gw[:, 3 * D:] = dot_nn(hidt[...], gp[...]).astype(BF16)
    hidt[...] = hid[...].T
    for b in range(3):
        cs = pl.ds(b * D, D)
        gw[:, cs] = dot_nn(hidt[...], dproj[:, cs]).astype(BF16)

    gp[...] = dot_nt(dproj[...], wqkv[...]).astype(BF16)

    def phase_f(i, c):
        r = pl.ds(pl.multiple_of(i * CH, CH), CH)
        x = tok[r, :].astype(F32)
        xc, rs = ln_stats(x)
        xh = xc * rs
        gm = gp[r, :].astype(F32) * (1.0 + scale[...])
        gx = rs * (gm - jnp.mean(gm, axis=-1, keepdims=True)
                   - xh * jnp.mean(gm * xh, axis=-1, keepdims=True))
        gtok[r, :] = (cot[r, :].astype(F32) + gx).astype(BF16)
        return c

    lax.fori_loop(0, n // CH, phase_f, 0)


def compute(tok, cot, shift, scale, gate, wqkv, wo, qg, kg):
    n = tok.shape[0]
    vm = pl.BlockSpec(memory_space=pltpu.VMEM)
    return pl.pallas_call(
        compute_kernel,
        out_shape=(
            jax.ShapeDtypeStruct((n, D), BF16),
            jax.ShapeDtypeStruct((n, D), BF16),
            jax.ShapeDtypeStruct((D, 4 * D), BF16),
        ),
        in_specs=[vm] * 9,
        out_specs=(vm,) * 3,
        scratch_shapes=[
            pltpu.VMEM((n, D), BF16),
            pltpu.VMEM((n, 3 * D), BF16),
            pltpu.VMEM((n, D), BF16),
            pltpu.VMEM((n, D), BF16),
            pltpu.VMEM((n, D), BF16),
            pltpu.VMEM((n, 3 * D), BF16),
            pltpu.VMEM((D, n), BF16),
        ],
        compiler_params=pltpu.CompilerParams(vmem_limit_bytes=56 * 1024 * 1024),
        cost_estimate=pl.CostEstimate(flops=2 * n * D * 12 * D, bytes_accessed=30 * 2**20, transcendentals=0),
    )(tok, cot, shift, scale, gate, wqkv, wo, qg, kg)


def to_groups(x):
    y = lax.all_to_all(x[0], "seq", split_axis=1, concat_axis=0, tiled=True)
    f, p, d = y.shape
    return y.reshape(f, p // 16, 16, d).transpose(1, 0, 2, 3).reshape(f * p, d)


def from_groups(y, frames, pos):
    z = y.reshape(pos // 16, frames, 16, D).transpose(1, 0, 2, 3).reshape(frames, pos, D)
    return lax.all_to_all(z, "seq", split_axis=0, concat_axis=1, tiled=True)[None]


def on_device(tokens, mod_shift, mod_scale, res_gate, qkv_weight, out_weight, query_gain, key_gain, cotangent):
    tok = to_groups(tokens)
    cot = to_groups(cotangent)
    n = tok.shape[0]
    out, gtok, gw = compute(tok, cot, mod_shift, mod_scale, res_gate, qkv_weight, out_weight,
                            query_gain[None], key_gain[None])
    block_output = from_groups(out, 16, n // 16)
    grad_tokens = from_groups(gtok, 16, n // 16)
    summed = lax.psum_scatter(gw, ("dp", "seq"), scatter_dimension=0, tiled=True)
    return block_output, grad_tokens, summed[:, : 3 * D], summed[:, 3 * D :]


def solution(mesh):
    tok = P("dp", "seq", None, None)
    vec = P("dp", None)
    return jax.shard_map(
        on_device,
        mesh=mesh,
        in_specs=(tok, vec, vec, vec, P(), P(), P(), P(), tok),
        out_specs=(tok, tok, P(("dp", "seq"), None), P(("dp", "seq"), None)),
        check_vma=False,
    )
```

time: 472 us -> 370 us (0.78)
  blocking collectives: 143 us -> 0 us
  waiting for transfers between devices: 82.6 us -> 202 us
  Pallas kernels: 0 us -> 109 us
  local copies, waits for them, and re-layouts: 88.4 us -> 17.3 us
  matrix products: 65.4 us -> 0 us
  other arithmetic: 46.7 us -> 0 us
  starting transfers between devices: 35.4 us -> 21.1 us
  between operations: 1.72 us -> 14.5 us
    unnamed x1 -> x0, blocking collectives: 143 us -> none
    unnamed x0 -> x2, waiting for transfers between devices: none -> 134 us
    pallas_call x0 -> x1, Pallas kernels: none -> 109 us  [compute(): pl.pallas_call(compute_kernel, out_shape=(jax.ShapeDtypeStruct((n, D), BF...]
    dot_general x12 -> x0, matrix products: 65.4 us -> none  [the longest x3 20.6 us: attend(): jnp.einsum('vfphd,vgphd->vphfg', query_norm, key_norm, preferred_element_...]
    convert_element_type x11 -> x0, local copies, waits for them, and re-layouts: 44.4 us -> none  [the longest x6 28.4 us: rms_gain(): as_float = inputs.astype(jnp.float32)]
    convert_element_type x7 -> x0, other arithmetic: 23 us -> none  [the longest x3 14 us: rms_gain(): as_float = inputs.astype(jnp.float32)]
    reshape x4 -> x2, local copies, waits for them, and re-layouts: 19.7 us -> 2.28 us  [from_groups(): y.reshape(pos // 16, frames, 16, D).transpose(1, 0, 2, 3)]
    all_to_all x4, waiting for transfers between devices: 82.6 us -> 67.7 us  [the longest x2 36.2 us: from_groups(): lax.all_to_all(z, 'seq', split_axis=0, concat_axis=1, tiled=True)[None]]
  transfers between devices with their start and end apart: 4 -> 5, of which waited for: 2 -> 5; matrix products, arithmetic and copies ran while one was open for 22% -> 2% of each run, Pallas kernels for 0% -> 0%
where the time goes in v1:
time: 370 us; the launch traced here: 363 us
  waiting for transfers between devices  202 us (55%)
  Pallas kernels  109 us (29%)
  starting transfers between devices  21.1 us (6%)
  local copies, waits for them, and re-layouts  17.3 us (5%)
  between operations  14.5 us (4%)
    unnamed x2, waiting for transfers between devices  134 us
    pallas_call x1, Pallas kernels, compute(): pl.pallas_call(compute_kernel, out_shape=(jax.ShapeDtypeStruct((n, D), BF...  109 us
    all_to_all x2, waiting for transfers between devices, from_groups(): lax.all_to_all(z, 'seq', split_axis=0, concat_axis=1, tiled=True)[None]  36.2 us
    all_to_all x2, waiting for transfers between devices, to_groups(): y = lax.all_to_all(x[0], 'seq', split_axis=1, concat_axis=0, tiled=True)  31.5 us
    all_to_all x2, starting transfers between devices, to_groups(): y = lax.all_to_all(x[0], 'seq', split_axis=1, concat_axis=0, tiled=True)  11.4 us
    all_to_all x2, starting transfers between devices, from_groups(): lax.all_to_all(z, 'seq', split_axis=0, concat_axis=1, tiled=True)[None]  9.68 us
  transfers between devices with their start and end apart: 5, of which 5 were waited for; matrix products, arithmetic and copies ran while one was open for 2% of the time, Pallas kernels for 0%

profile of v1, /device:TPU:0, one launch (start us, length us, event | category | flops | bytes accessed | tf_op | source)
XLA Modules:
  0.0 362.9 jit_solution(3066962568721640730)
XLA Ops:
  7.2 3.5 copy.40
  10.7 0.0 copy-start
  10.7 7.8 %all-to-all-start = ((bf16[2,256,1152]{2,0,1:T(2,128)(2,1)}), bf16[2,256,1152]{2,0,1:T(2,128)(2,1)S(1)}, u32[]{:S(2)}, u32[]{:S(2)}) async-start(bf16[2,256,1152]{2,0,1:T(2,128)(2,1)} %bitcast.37), calls=%async_computation | async-start | bytes 2359296 | tf_op jit(solution)/shard_map/all_to_all | solution.py:150
  18.5 0.0 copy-done
  18.5 2.2 copy.39
  20.7 15.7 %all-to-all-done = bf16[2,256,1152]{2,0,1:T(2,128)(2,1)S(1)} async-done(((bf16[2,256,1152]{2,0,1:T(2,128)(2,1)}), bf16[2,256,1152]{2,0,1:T(2,128)(2,1)S(1)}, u32[]{:S(2)}, u32[]{:S(2)}) %all-to-all-start) | async-done | bytes 1179680 | tf_op jit(solution)/shard_map/all_to_all | solution.py:150
  36.4 3.6 all-to-all-start.1
  40.0 0.0 all-reduce.3.cloned.1.call-start
  40.0 0.1 copy.26
  40.2 0.1 copy.27
  40.3 1.1 copy.28
  41.4 15.8 %all-to-all-done.1 = bf16[2,256,1152]{2,0,1:T(2,128)(2,1)S(1)} async-done(((bf16[2,256,1152]{2,0,1:T(2,128)(2,1)}), bf16[2,256,1152]{2,0,1:T(2,128)(2,1)S(1)}, u32[]{:S(2)}, u32[]{:S(2)}) %all-to-all-start.1) | async-done | bytes 1179680 | tf_op jit(solution)/shard_map/all_to_all | solution.py:150
  57.2 0.1 copy.30
  57.4 0.1 copy.31
  57.5 1.1 copy.32
  58.6 108.5 %shard_map.120 = (bf16[512,1152]{1,0:T(8,128)(2,1)}, bf16[512,1152]{1,0:T(8,128)(2,1)}, bf16[1152,4608]{1,0:T(8,128)(2,1)}) custom-call(bf16[512,1152]{1,0:T(8,128)(2,1)} %bitcast.47, bf16[512,1152]{1,0:T(8,128)(2,1)} %bitcast.49, f32[1,1152]{1,0:T(1,128)} %shift.1, f32[1,1152]{1,0:T(1,128)} %scale.1, f32[1,1152]{1,0:T(1,128)} %gate.1, ...), custom_call_target="tpu_custom_call" | custom-call | flops 16307453952 | bytes 31457280 | tf_op jit(solution)/shard_map/pallas_call | solution.py:126
  167.1 0.0 copy-start.2
  167.1 0.0 all-reduce.3.cloned.1.call-update
  167.1 1.2 copy-done.2
  168.4 1.1 copy.33
  169.5 0.0 copy-start.1
  169.5 3.9 %all-to-all-start.2 = ((bf16[16,32,1152]{2,1,0:T(8,128)(2,1)}), bf16[16,32,1152]{2,1,0:T(8,128)(2,1)S(1)}, u32[]{:S(2)}, u32[]{:S(2)}) async-start(bf16[16,32,1152]{2,1,0:T(8,128)(2,1)} %bitcast.16), calls=%async_computation.2 | async-start | bytes 2359296 | tf_op jit(solution)/shard_map/all_to_all | solution.py:157
  173.4 0.0 copy-done.1
  173.4 1.2 copy.35
  174.6 18.7 %all-to-all-done.2 = bf16[16,32,1152]{2,1,0:T(8,128)(2,1)S(1)} async-done(((bf16[16,32,1152]{2,1,0:T(8,128)(2,1)}), bf16[16,32,1152]{2,1,0:T(8,128)(2,1)S(1)}, u32[]{:S(2)}, u32[]{:S(2)}) %all-to-all-start.2) | async-done | bytes 1179680 | tf_op jit(solution)/shard_map/all_to_all | solution.py:157
  193.3 5.7 %all-to-all-start.3 = ((bf16[16,32,1152]{2,1,0:T(8,128)(2,1)}), bf16[16,32,1152]{2,1,0:T(8,128)(2,1)S(1)}, u32[]{:S(2)}, u32[]{:S(2)}) async-start(bf16[16,32,1152]{2,1,0:T(8,128)(2,1)} %bitcast.22), calls=%async_computation.3 | async-start | bytes 2359296 | tf_op jit(solution)/shard_map/all_to_all | solution.py:157
  199.0 1.1 copy.34
  200.2 17.5 %all-to-all-done.3 = bf16[16,32,1152]{2,1,0:T(8,128)(2,1)S(1)} async-done(((bf16[16,32,1152]{2,1,0:T(8,128)(2,1)}), bf16[16,32,1152]{2,1,0:T(8,128)(2,1)S(1)}, u32[]{:S(2)}, u32[]{:S(2)}) %all-to-all-start.3) | async-done | bytes 1179680 | tf_op jit(solution)/shard_map/all_to_all | solution.py:157
  217.6 1.1 copy.36
  218.7 133.8 %all-reduce.3.cloned.1.call-done = bf16[1152,4608]{1,0:T(8,128)(2,1)} async-done(((bf16[1152,4608]{1,0:T(8,128)(2,1)}), bf16[1152,4608]{1,0:T(8,128)(2,1)}) %all-reduce.3.cloned.1.call-update) | async-done | bytes 10616848
  352.5 1.6 constant_dynamic-slice_fusion
  354.1 1.5 dynamic-slice.2
Async XLA Ops:
  10.7 7.8 %copy-start = (bf16[1,2,256,1152]{3,2,1,0:T(8,128)(2,1)S(1)}, bf16[1,2,256,1152]{3,2,1,0:T(8,128)(2,1)}, u32[]{:S(2)}) copy-start(bf16[1,2,256,1152]{3,2,1,0:T(8,128)(2,1)} %param.17) | copy-start | bytes 3538948
  10.7 25.7 %all-to-all-start = ((bf16[2,256,1152]{2,0,1:T(2,128)(2,1)}), bf16[2,256,1152]{2,0,1:T(2,128)(2,1)S(1)}, u32[]{:S(2)}, u32[]{:S(2)}) async-start(bf16[2,256,1152]{2,0,1:T(2,128)(2,1)} %bitcast.37), calls=%async_computation | async-start | bytes 2359296 | tf_op jit(solution)/shard_map/all_to_all | solution.py:150
  36.4 20.8 %all-to-all-start.1 = ((bf16[2,256,1152]{2,0,1:T(2,128)(2,1)}), bf16[2,256,1152]{2,0,1:T(2,128)(2,1)S(1)}, u32[]{:S(2)}, u32[]{:S(2)}) async-start(bf16[2,256,1152]{2,0,1:T(2,128)(2,1)} %bitcast.36), calls=%async_computation.1 | async-start | bytes 2359296 | tf_op jit(solution)/shard_map/all_to_all | solution.py:150
  40.0 312.6 %all-reduce.3.cloned.1.call-start = ((), (), s32[]{:S(2)}) async-start(), calls=%async_computation.4 | async-start | bytes 21233664
  167.1 1.3 copy-start.2
  169.5 4.0 %copy-start.1 = (bf16[512,1152]{1,0:T(8,128)(2,1)S(1)}, bf16[512,1152]{1,0:T(8,128)(2,1)}, u32[]{:S(2)}) copy-start(bf16[512,1152]{1,0:T(8,128)(2,1)} %get-tuple-element.8) | copy-start | bytes 3538948
  169.5 23.8 %all-to-all-start.2 = ((bf16[16,32,1152]{2,1,0:T(8,128)(2,1)}), bf16[16,32,1152]{2,1,0:T(8,128)(2,1)S(1)}, u32[]{:S(2)}, u32[]{:S(2)}) async-start(bf16[16,32,1152]{2,1,0:T(8,128)(2,1)} %bitcast.16), calls=%async_computation.2 | async-start | bytes 2359296 | tf_op jit(solution)/shard_map/all_to_all | solution.py:157
  193.3 24.3 %all-to-all-start.3 = ((bf16[16,32,1152]{2,1,0:T(8,128)(2,1)}), bf16[16,32,1152]{2,1,0:T(8,128)(2,1)S(1)}, u32[]{:S(2)}, u32[]{:S(2)}) async-start(bf16[16,32,1152]{2,1,0:T(8,128)(2,1)} %bitcast.22), calls=%async_computation.3 | async-start | bytes 2359296 | tf_op jit(solution)/shard_map/all_to_all | solution.py:157
Sparse Core Ops, SparseCore 0:
  167.3 185.2 all-reduce.2

commit v2 on v1

v2 whole, which is shorter than its diff:
```python
import numpy as np
import jax
import jax.numpy as jnp
from jax import lax
from jax.experimental import pallas as pl
from jax.experimental.pallas import tpu as pltpu
from jax.sharding import PartitionSpec as P

F32 = jnp.float32
BF16 = jnp.bfloat16
D = 1152
MESH = pl.DeviceIdType.MESH
PARTS = 4
ORDERS = ((1, 0, 2), (0, 2, 1), (2, 1, 0), (1, 2, 0))
RA, RB = 80, 64


def natural_rows():
    i = np.arange(D)
    core, rest = i // 576, i % 576
    a = (rest // 144, (rest // 36) % 4, (rest // 9) % 4)
    j = rest % 9
    table = np.zeros((D, PARTS), np.int32)
    for p, order in enumerate(ORDERS):
        c = [None] * 3
        for place, dim in enumerate(order):
            c[dim] = a[place]
        x, y, z = c
        table[:, p] = 9 * ((z % 2) * 64 + y * 16 + core * 8 + x * 2 + z // 2) + j
    return table


def spread(rows_from, rows_to):
    m = np.zeros((4 * rows_to, 4 * rows_from), np.float32)
    for b in range(4):
        for j in range(rows_from):
            m[b * rows_to + j, b * rows_from + j] = 1.0
    return m


def coords():
    dp = lax.axis_index("dp")
    sq = lax.axis_index("seq")
    z = lax.rem(sq, 2) * 2 + dp // 8
    return (sq // 2, lax.rem(dp // 2, 4), z), lax.rem(dp, 2)


def device(xyz, core):
    x, y, z = xyz
    return (lax.rem(z, 2) * 8 + y * 2 + core, x * 2 + z // 2)


def shifted(xyz, dim, k):
    out = list(xyz)
    out[dim] = lax.rem(xyz[dim] + k, 4)
    return tuple(out)


def dot_nn(a, b):
    return lax.dot_general(a, b, (((1,), (0,)), ((), ())), preferred_element_type=F32)


class Reduce:
    def __init__(self, p, xyz, core, g, fa, fb, fl, fr, s2, r2, s3, r3, send, recv):
        self.p, self.xyz, self.core = p, xyz, core
        self.g, self.fa, self.fb, self.fl, self.fr = g, fa, fb, fl, fr
        self.s2, self.r2, self.s3, self.r3 = s2, r2, s3, r3
        self.send, self.recv = send, recv
        self.sent = []

    def copy(self, i, src, dst, xyz):
        c = pltpu.make_async_remote_copy(
            src_ref=src, dst_ref=dst, send_sem=self.send.at[self.p, i], recv_sem=self.recv.at[self.p, i],
            device_id=device(xyz, self.core), device_id_type=MESH)
        c.start()
        self.sent.append(c)
        return c

    def at(self, k, lo, n):
        start = pl.multiple_of(lax.rem(self.xyz[ORDERS[self.p][0]] + k, 4) * 144 + lo, 16)
        return pl.ds(start, n)

    def start(self):
        p, d = self.p, ORDERS[self.p][0]
        right, left = shifted(self.xyz, d, 1), shifted(self.xyz, d, 3)
        self.c0 = self.copy(0, self.g.at[p, self.at(2, 0, RA)], self.fa.at[p], right)
        self.c1 = self.copy(1, self.g.at[p, self.at(2, RA, RB)], self.fb.at[p], left)
        self.c2 = self.copy(2, self.g.at[p, self.at(1, RA, RB)], self.fl.at[p, pl.ds(RA, RB)], right)
        self.c3 = self.copy(3, self.g.at[p, self.at(3, 0, RA)], self.fr.at[p, pl.ds(0, RA)], left)

    def forward(self):
        p, d = self.p, ORDERS[self.p][0]
        right, left = shifted(self.xyz, d, 1), shifted(self.xyz, d, 3)
        self.c0.wait_recv()
        r = self.at(1, 0, RA)
        self.g[p, r] = (self.g[p, r].astype(F32) + self.fa[p].astype(F32)).astype(BF16)
        self.c4 = self.copy(4, self.g.at[p, r], self.fl.at[p, pl.ds(0, RA)], right)
        self.c1.wait_recv()
        r = self.at(3, RA, RB)
        self.g[p, r] = (self.g[p, r].astype(F32) + self.fb[p].astype(F32)).astype(BF16)
        self.c5 = self.copy(5, self.g.at[p, r], self.fr.at[p, pl.ds(RA, RB)], left)

    def second(self, pad2):
        p, d = self.p, ORDERS[self.p][1]
        for c in (self.c2, self.c3, self.c4, self.c5):
            c.wait_recv()
        r = self.at(0, 0, 144)
        total = self.g[p, r].astype(F32) + self.fl[p].astype(F32) + self.fr[p].astype(F32)
        self.s2[p] = dot_nn(pad2[...], total.astype(BF16)).astype(BF16)
        self.cs2 = []
        for k in (2, 1, 3):
            peer = shifted(self.xyz, d, k)
            rows = pl.ds(pl.multiple_of(peer[d] * 48, 16), 48)
            self.cs2.append(self.copy(5 + k, self.s2.at[p, rows], self.r2.at[p, k - 1], peer))

    def third(self, pad3):
        p, d = self.p, ORDERS[self.p][2]
        for c in self.cs2:
            c.wait_recv()
        rows = pl.ds(pl.multiple_of(self.xyz[ORDERS[p][1]] * 48, 16), 48)
        total = self.s2[p, rows].astype(F32)
        for k in range(3):
            total = total + self.r2[p, k].astype(F32)
        self.s3[p] = dot_nn(pad3[...], total.astype(BF16)).astype(BF16)
        self.cs3 = []
        for k in (2, 1, 3):
            peer = shifted(self.xyz, d, k)
            rows = pl.ds(pl.multiple_of(peer[d] * 16, 16), 16)
            self.cs3.append(self.copy(8 + k, self.s3.at[p, rows], self.r3.at[p, k - 1], peer))

    def finish(self):
        p = self.p
        for c in self.cs3:
            c.wait_recv()
        rows = pl.ds(pl.multiple_of(self.xyz[ORDERS[p][2]] * 16, 16), 16)
        total = self.s3[p, rows].astype(F32)
        for k in range(3):
            total = total + self.r3[p, k].astype(F32)
        for c in self.sent:
            c.wait_send()
        return total[:9].astype(BF16)


def reduce_scratch():
    return [
        pltpu.VMEM((PARTS, 576, D), BF16),
        pltpu.VMEM((PARTS, RA, D), BF16),
        pltpu.VMEM((PARTS, RB, D), BF16),
        pltpu.VMEM((PARTS, 144, D), BF16),
        pltpu.VMEM((PARTS, 144, D), BF16),
        pltpu.VMEM((PARTS, 192, D), BF16),
        pltpu.VMEM((PARTS, 3, 48, D), BF16),
        pltpu.VMEM((PARTS, 64, D), BF16),
        pltpu.VMEM((PARTS, 3, 16, D), BF16),
        pltpu.SemaphoreType.DMA((PARTS, 12)),
        pltpu.SemaphoreType.DMA((PARTS, 12)),
    ]


def partners(xyz, core):
    out = [device(shifted(xyz, d, k), core) for d in range(3) for k in (1, 2, 3)]
    out.append(device(xyz, 1 - core))
    return out


def entry_barrier(devices):
    sem = pltpu.get_barrier_semaphore()
    for dev in devices:
        pl.semaphore_signal(sem, inc=1, device_id=dev, device_id_type=MESH)
    pl.semaphore_wait(sem, len(devices))


def rs_kernel(gw, pad2, pad3, outq, outo, pair, psend, precv, *scratch):
    xyz, core = coords()
    entry_barrier(partners(xyz, core))
    g = scratch[0]
    pairs = []
    for p in range(PARTS):
        other = pl.ds(pl.multiple_of((1 - core) * 576, 576), 576)
        c = pltpu.make_async_remote_copy(
            src_ref=gw.at[p, other], dst_ref=pair.at[p], send_sem=psend.at[p], recv_sem=precv.at[p],
            device_id=device(xyz, 1 - core), device_id_type=MESH)
        c.start()
        pairs.append(c)
    parts = [Reduce(p, xyz, core, *scratch) for p in range(PARTS)]
    for p in range(PARTS):
        pairs[p].wait_recv()

        def add(i, c, p=p):
            r = pl.ds(pl.multiple_of(i * 16, 16), 16)
            mine = pl.ds(pl.multiple_of(core * 576 + i * 16, 16), 16)
            g[p, r] = (gw[p, mine].astype(F32) + pair[p, r].astype(F32)).astype(BF16)
            return c

        lax.fori_loop(0, 36, add, 0)
        parts[p].start()
    for r in parts:
        r.forward()
    for r in parts:
        r.second(pad2)
    for r in parts:
        r.third(pad3)
    for p in range(3):
        outq[:, p * D:(p + 1) * D] = parts[p].finish()
    outo[...] = parts[3].finish()
    for c in pairs:
        c.wait_send()


def reduce_scatter(gw):
    vm = pl.BlockSpec(memory_space=pltpu.VMEM)
    pad2 = jnp.asarray(spread(36, 48), BF16)
    pad3 = jnp.asarray(np.pad(spread(9, 16), ((0, 0), (0, 12))), BF16)
    return pl.pallas_call(
        rs_kernel,
        out_shape=(jax.ShapeDtypeStruct((9, 3 * D), BF16), jax.ShapeDtypeStruct((9, D), BF16)),
        in_specs=[vm] * 3,
        out_specs=(vm, vm),
        scratch_shapes=[pltpu.VMEM((PARTS, 576, D), BF16), pltpu.SemaphoreType.DMA((PARTS,)),
                        pltpu.SemaphoreType.DMA((PARTS,))] + reduce_scratch(),
        compiler_params=pltpu.CompilerParams(collective_id=0, has_side_effects=True, vmem_limit_bytes=56 * 1024 * 1024),
        cost_estimate=pl.CostEstimate(flops=10**9, bytes_accessed=20 * 2**20, transcendentals=0),
    )(gw, pad2, pad3)


HD = 72
NH = 16
GR = 256
N = 512


def dot_nt(a, b):
    return lax.dot_general(a, b, (((1,), (1,)), ((), ())), preferred_element_type=F32)


def dot_tn(a, b):
    return lax.dot_general(a, b, (((0,), (0,)), ((), ())), preferred_element_type=F32)


def group_rows(g):
    if isinstance(g, int):
        return pl.ds(g * GR, GR)
    return pl.ds(pl.multiple_of(g * GR, GR), GR)


def sub_rows(g, i, n):
    return pl.ds(pl.multiple_of(g * GR + i * n, n), n)


LN_CH = 64


def ln_forward(g, tok, shift, scale, xh, rstd, hid):
    def body(i, c):
        r = sub_rows(g, i, LN_CH)
        x = tok[r, :].astype(F32)
        xc = x - jnp.mean(x, axis=-1, keepdims=True)
        rs = lax.rsqrt(jnp.mean(xc * xc, axis=-1, keepdims=True) + 1e-6)
        n = xc * rs
        xh[r, :] = n
        rstd[r, :] = jnp.broadcast_to(rs, (LN_CH, 128))
        hid[r, :] = (n * (1.0 + scale[...]) + shift[...]).astype(BF16)
        return c

    lax.fori_loop(0, GR // LN_CH, body, 0, unroll=2)


def ln_backward(g, gh, cot, scale, xh, rstd, gtok):
    def body(i, c):
        r = sub_rows(g, i, LN_CH)
        n = xh[r, :]
        gm = gh[r, :].astype(F32) * (1.0 + scale[...])
        m1 = jnp.mean(gm, axis=-1, keepdims=True)
        m2 = jnp.mean(gm * n, axis=-1, keepdims=True)
        gx = rstd[r, :1] * (gm - m1 - n * m2)
        gtok[r, :] = (cot[r, :].astype(F32) + gx).astype(BF16)
        return c

    lax.fori_loop(0, GR // LN_CH, body, 0, unroll=2)


def head_sum(x, ones_in):
    return dot_nn(x.astype(BF16), ones_in[...]) * (1.0 / HD)


def head_spread(m, ones_out):
    hi = m.astype(BF16)
    lo = (m - hi.astype(F32)).astype(BF16)
    return dot_nn(hi, ones_out[...]) + dot_nn(lo, ones_out[...])


def norm_forward(g, proj, qg, kg, qn, kn, ones_in, ones_out):
    r = group_rows(g)
    for col, gain, dst in ((0, qg, qn), (D, kg, kn)):
        x = proj[r, pl.ds(col, D)].astype(F32)
        ms = head_sum(x * x, ones_in)
        inv = head_spread(lax.rsqrt(ms + 1e-6), ones_out)
        dst[r, :] = (x * inv * gain[...]).astype(BF16)


def norm_backward(g, proj, qg, kg, dqn, dkn, ones_in, ones_out):
    r = group_rows(g)
    for col, gain, dn in ((0, qg, dqn), (D, kg, dkn)):
        x = proj[r, pl.ds(col, D)].astype(F32)
        inv = head_spread(lax.rsqrt(head_sum(x * x, ones_in) + 1e-6), ones_out)
        xh = x * inv
        d = dn[r, :].astype(F32) * gain[...]
        m = head_spread(head_sum(d * xh, ones_in), ones_out)
        proj[r, pl.ds(col, D)] = (inv * (d - xh * m)).astype(BF16)


def head_window(h):
    lo, hi = h * HD, (h + 1) * HD
    t0, t1 = lo // 128, (hi - 1) // 128
    return t0, t1 + 1, lo - t0 * 128, hi - t0 * 128


def lane_mask(lo, hi, w):
    lane = lax.broadcasted_iota(jnp.int32, (1, w), 1)
    return (lane >= lo) & (lane < hi)


def pick(x, lo, hi):
    w = x.shape[1]
    lane = lax.broadcasted_iota(jnp.int32, x.shape, 1)
    return jnp.where((lane >= lo) & (lane < hi), x, jnp.zeros_like(x))


def block_mask():
    ri = lax.broadcasted_iota(jnp.int32, (GR, GR), 0)
    ci = lax.broadcasted_iota(jnp.int32, (GR, GR), 1)
    return (ri & 15) == (ci & 15)


class Tiles:
    def __init__(self, ref, r, col):
        self.ref, self.r, self.col, self.part = ref, r, col, {}

    def add(self, h, val):
        t0, t1, lo, hi = head_window(h)
        for t in range(t0, t1):
            piece = val[:, (t - t0) * 128:(t - t0 + 1) * 128]
            if t in self.part:
                lane = lax.broadcasted_iota(jnp.int32, piece.shape, 1)
                piece = jnp.where(lane >= h * HD - t * 128, piece, self.part.pop(t))
            if (h + 1) * HD >= (t + 1) * 128:
                self.ref[self.r, pl.ds(self.col + t * 128, 128)] = piece.astype(BF16)
            else:
                self.part[t] = piece


def att_forward(g, proj, qn, kn, att, prob):
    r = group_rows(g)
    mask = block_mask()
    out = Tiles(att, r, 0)
    for h in range(NH):
        t0, t1, lo, hi = head_window(h)
        w = pl.ds(t0 * 128, (t1 - t0) * 128)
        q = pick(qn[r, w], lo, hi)
        s = dot_nt(q, kn[r, w])
        e = jnp.where(mask, jnp.exp(s), 0.0)
        p = (e * (1.0 / jnp.sum(e, axis=-1, keepdims=True))).astype(BF16)
        prob[g, h] = p
        out.add(h, dot_nn(p, proj[r, pl.ds(2 * D + t0 * 128, (t1 - t0) * 128)]))


def att_backward(g, proj, qn, kn, att, gatt, prob, ones_in):
    r = group_rows(g)
    delta = head_sum(gatt[r, :].astype(F32) * att[r, :].astype(F32) * HD, ones_in)
    odq, odk, odv = Tiles(qn, r, 0), Tiles(kn, r, 0), Tiles(proj, r, 2 * D)
    for h in range(NH):
        t0, t1, lo, hi = head_window(h)
        w = pl.ds(t0 * 128, (t1 - t0) * 128)
        da = gatt[r, w]
        q, k = qn[r, w], kn[r, w]
        dp = dot_nt(pick(da, lo, hi), proj[r, pl.ds(2 * D + t0 * 128, (t1 - t0) * 128)])
        p = prob[g, h]
        ds = (p.astype(F32) * (dp - delta[:, h:h + 1])).astype(BF16)
        odv.add(h, dot_tn(p, da))
        odq.add(h, dot_nn(ds, k))
        odk.add(h, dot_tn(ds, q))


def out_projection(g, tok, att, wo, gate, out):
    r = group_rows(g)
    out[r, :] = (tok[r, :].astype(F32) + gate[...] * dot_nn(att[r, :], wo[...])).astype(BF16)


def grad_att(g, cot, gate, wo, gp, gatt):
    r = group_rows(g)
    x = (cot[r, :].astype(F32) * gate[...]).astype(BF16)
    gp[r, :] = x
    gatt[r, :] = dot_nt(x, wo[...]).astype(BF16)


PCH = 192


def permuted_t(p, x, idx, xt):
    def body(i, c):
        r = pl.ds(pl.multiple_of(i * PCH, PCH), PCH)
        lane = lax.broadcasted_iota(jnp.int32, (PCH, D), 1)
        m = jnp.where(idx[r, p:p + 1] == lane, 1.0, 0.0).astype(BF16)
        xt[r, :] = dot_nt(m, x[...]).astype(BF16)
        return c

    lax.fori_loop(0, D // PCH, body, 0)


def solo_kernel(tok, cot, shift, scale, gate, wqkv, wo, qg, kg, idx, ones_in, ones_out, out, gtok, gw,
                hid, xh, rstd, proj, qn, kn, att, prob, gp, gatt, xt):
    for g in range(2):
        ln_forward(g, tok, shift, scale, xh, rstd, hid)
        r = group_rows(g)
    for b in range(3):
        cs = pl.ds(b * D, D)
        proj[:, cs] = dot_nn(hid[...], wqkv[:, cs]).astype(BF16)
    for g in range(2):
        norm_forward(g, proj, qg, kg, qn, kn, ones_in, ones_out)

    def fwd(g, c):
        att_forward(g, proj, qn, kn, att, prob)
        return c

    lax.fori_loop(0, 2, fwd, 0)
    for g in range(2):
        out_projection(g, tok, att, wo, gate, out)
        grad_att(g, cot, gate, wo, gp, gatt)

    permuted_t(3, att, idx, xt)
    gw[3] = dot_nn(xt[...], gp[...]).astype(BF16)

    def bwd(g, c):
        att_backward(g, proj, qn, kn, att, gatt, prob, ones_in)
        return c

    lax.fori_loop(0, 2, bwd, 0)
    for g in range(2):
        norm_backward(g, proj, qg, kg, qn, kn, ones_in, ones_out)
    for b in range(3):
        permuted_t(b, hid, idx, xt)
        gw[b] = dot_nn(xt[...], proj[:, pl.ds(b * D, D)]).astype(BF16)
    gatt[...] = dot_nt(proj[...], wqkv[...]).astype(BF16)
    for g in range(2):
        ln_backward(g, gatt, cot, scale, xh, rstd, gtok)


def ones_matrices():
    a = np.zeros((D, 128), np.float32)
    b = np.zeros((128, D), np.float32)
    for h in range(NH):
        a[h * HD:(h + 1) * HD, h] = 1.0
        b[h, h * HD:(h + 1) * HD] = 1.0
    return a, b


def compute(tok, cot, shift, scale, gate, wqkv, wo, qg, kg):
    vm = pl.BlockSpec(memory_space=pltpu.VMEM)
    a, b = ones_matrices()
    qgf = jnp.tile(qg * HD ** -0.5, (1, NH))
    kgf = jnp.tile(kg, (1, NH))
    return pl.pallas_call(
        solo_kernel,
        out_shape=(
            jax.ShapeDtypeStruct((N, D), BF16),
            jax.ShapeDtypeStruct((N, D), BF16),
            jax.ShapeDtypeStruct((4, D, D), BF16),
        ),
        in_specs=[vm] * 12,
        out_specs=(vm,) * 3,
        scratch_shapes=[
            pltpu.VMEM((N, D), BF16),
            pltpu.VMEM((N, D), F32),
            pltpu.VMEM((N, 128), F32),
            pltpu.VMEM((N, 3 * D), BF16),
            pltpu.VMEM((N, D), BF16),
            pltpu.VMEM((N, D), BF16),
            pltpu.VMEM((N, D), BF16),
            pltpu.VMEM((2, NH, GR, GR), BF16),
            pltpu.VMEM((N, D), BF16),
            pltpu.VMEM((N, D), BF16),
            pltpu.VMEM((D, N), BF16),
        ],
        compiler_params=pltpu.CompilerParams(vmem_limit_bytes=62 * 1024 * 1024),
    )(tok, cot, shift, scale, gate, wqkv, wo, qgf, kgf, jnp.asarray(natural_rows()),
      jnp.asarray(a, BF16), jnp.asarray(b, BF16))


def to_groups(x):
    y = lax.all_to_all(x[0], "seq", split_axis=1, concat_axis=0, tiled=True)
    f, p, d = y.shape
    return y.reshape(f, p // 16, 16, d).transpose(1, 0, 2, 3).reshape(f * p, d)


def from_groups(y, frames, pos):
    z = y.reshape(pos // 16, frames, 16, D).transpose(1, 0, 2, 3).reshape(frames, pos, D)
    return lax.all_to_all(z, "seq", split_axis=0, concat_axis=1, tiled=True)[None]


def on_device(tokens, mod_shift, mod_scale, res_gate, qkv_weight, out_weight, query_gain, key_gain, cotangent):
    tok = to_groups(tokens)
    cot = to_groups(cotangent)
    n = tok.shape[0]
    out, gtok, gw = compute(tok, cot, mod_shift, mod_scale, res_gate, qkv_weight, out_weight,
                            query_gain[None], key_gain[None])
    block_output = from_groups(out, 16, n // 16)
    grad_tokens = from_groups(gtok, 16, n // 16)
    grad_qkv_weight, grad_out_weight = reduce_scatter(gw)
    return block_output, grad_tokens, grad_qkv_weight, grad_out_weight


def solution(mesh):
    tok = P("dp", "seq", None, None)
    vec = P("dp", None)
    return jax.shard_map(
        on_device,
        mesh=mesh,
        in_specs=(tok, vec, vec, vec, P(), P(), P(), P(), tok),
        out_specs=(tok, tok, P(("dp", "seq"), None), P(("dp", "seq"), None)),
        check_vma=False,
    )
```

time: 370 us -> 204 us (0.55)
  the two profiles are of different devices: /device:TPU:0 before, /device:TPU:1 now
where the time goes in v2:
time: 204 us; the launch traced here: 201 us
  Pallas kernels  117 us (57%)
  waiting for transfers between devices  44.8 us (22%)
  starting transfers between devices  21.1 us (10%)
  local copies, waits for them, and re-layouts  16.8 us (8%)
    pallas_call x1, Pallas kernels, compute(): pl.pallas_call(solo_kernel, out_shape=(jax.ShapeDtypeStruct((N, D), BF16)...  64.7 us
    pallas_call x1, Pallas kernels, reduce_scatter(): pl.pallas_call(rs_kernel, out_shape=(jax.ShapeDtypeStruct((9, 3 * D), BF1...  52.4 us
    all_to_all x2, waiting for transfers between devices, to_groups(): y = lax.all_to_all(x[0], 'seq', split_axis=1, concat_axis=0, tiled=True)  29.1 us
    all_to_all x2, waiting for transfers between devices, from_groups(): lax.all_to_all(z, 'seq', split_axis=0, concat_axis=1, tiled=True)[None]  15.7 us
    all_to_all x2, starting transfers between devices, to_groups(): y = lax.all_to_all(x[0], 'seq', split_axis=1, concat_axis=0, tiled=True)  12.9 us
    all_to_all x2, starting transfers between devices, from_groups(): lax.all_to_all(z, 'seq', split_axis=0, concat_axis=1, tiled=True)[None]  8.26 us
    unnamed x16, local copies, waits for them, and re-layouts  7.01 us
  transfers between devices with their start and end apart: 4, of which 3 were waited for; matrix products, arithmetic and copies ran while one was open for 4% of the time, Pallas kernels for 26%

profile of v2, /device:TPU:1, one launch (start us, length us, event | category | flops | bytes accessed | tf_op | source)
XLA Modules:
  0.0 200.8 jit_solution(16246764023526689151)
XLA Ops:
  0.6 3.5 %copy.45 = bf16[1,2,256,1152]{3,1,2,0:T(2,128)(2,1)} copy(bf16[1,2,256,1152]{3,2,1,0:T(8,128)(2,1)} %param.14) | data formatting | bytes 2359296 | tf_op args[0]
  4.1 0.0 copy-start
  4.1 8.3 %all-to-all-start = ((bf16[2,256,1152]{2,0,1:T(2,128)(2,1)}), bf16[2,256,1152]{2,0,1:T(2,128)(2,1)S(1)}, u32[]{:S(2)}, u32[]{:S(2)}) async-start(bf16[2,256,1152]{2,0,1:T(2,128)(2,1)} %bitcast.35), calls=%async_computation | async-start | bytes 2359296 | tf_op jit(solution)/shard_map/all_to_all | solution.py:490
  12.4 0.0 copy-done
  12.4 2.2 %copy.44 = bf16[1,2,256,1152]{3,1,2,0:T(2,128)(2,1)} copy(bf16[1,2,256,1152]{3,2,1,0:T(8,128)(2,1)S(1)} %copy-done) | data formatting | bytes 2359296 | tf_op args[8]
  14.7 15.0 %all-to-all-done = bf16[2,256,1152]{2,0,1:T(2,128)(2,1)S(1)} async-done(((bf16[2,256,1152]{2,0,1:T(2,128)(2,1)}), bf16[2,256,1152]{2,0,1:T(2,128)(2,1)S(1)}, u32[]{:S(2)}, u32[]{:S(2)}) %all-to-all-start) | async-done | bytes 1179680 | tf_op jit(solution)/shard_map/all_to_all | solution.py:490
  29.7 0.0 copy-start.5
  29.7 0.0 copy-start.4
  29.7 4.6 %all-to-all-start.1 = ((bf16[2,256,1152]{2,0,1:T(2,128)(2,1)}), bf16[2,256,1152]{2,0,1:T(2,128)(2,1)S(1)}, u32[]{:S(2)}, u32[]{:S(2)}) async-start(bf16[2,256,1152]{2,0,1:T(2,128)(2,1)} %bitcast.34), calls=%async_computation.1 | async-start | bytes 2359296 | tf_op jit(solution)/shard_map/all_to_all | solution.py:490
  34.2 0.0 copy-done.5
  34.3 0.7 tile.18.qg
  34.9 0.0 copy-done.4
  35.0 0.7 tile.20.kg
  35.6 0.1 copy.31
  35.8 0.1 copy.32
  35.9 1.1 copy.33
  37.0 14.0 %all-to-all-done.1 = bf16[2,256,1152]{2,0,1:T(2,128)(2,1)S(1)} async-done(((bf16[2,256,1152]{2,0,1:T(2,128)(2,1)}), bf16[2,256,1152]{2,0,1:T(2,128)(2,1)S(1)}, u32[]{:S(2)}, u32[]{:S(2)}) %all-to-all-start.1) | async-done | bytes 1179680 | tf_op jit(solution)/shard_map/all_to_all | solution.py:490
  51.1 0.1 copy.35
  51.2 0.1 copy.36
  51.3 1.1 copy.37
  52.4 64.7 %shard_map.165 = (bf16[512,1152]{1,0:T(8,128)(2,1)}, bf16[512,1152]{1,0:T(8,128)(2,1)}, bf16[4,1152,1152]{2,1,0:T(8,128)(2,1)}) custom-call(bf16[512,1152]{1,0:T(8,128)(2,1)} %bitcast.36, bf16[512,1152]{1,0:T(8,128)(2,1)} %bitcast.37, f32[1,1152]{1,0:T(1,128)} %shift.1, f32[1,1152]{1,0:T(1,128)} %scale.1, f32[1,1152]{1,0:T(1,128)} %gate.1, ...), custom_call_target="tpu_custom_call" | custom-call | tf_op jit(solution)/shard_map/pallas_call | solution.py:462
  117.2 2.4 %copy.40 = bf16[2,16,16,1152]{3,2,0,1:T(8,128)(2,1)} copy(bf16[2,16,16,1152]{3,2,1,0:T(8,128)(2,1)} %bitcast.47) | data formatting | bytes 2359296 | tf_op jit(solution)/shard_map/reshape | solution.py:496
  119.5 0.0 copy-start.1
  119.5 4.2 %all-to-all-start.3 = ((bf16[16,32,1152]{2,1,0:T(8,128)(2,1)}), bf16[16,32,1152]{2,1,0:T(8,128)(2,1)S(1)}, u32[]{:S(2)}, u32[]{:S(2)}) async-start(bf16[16,32,1152]{2,1,0:T(8,128)(2,1)} %bitcast.20), calls=%async_computation.3 | async-start | bytes 2359296 | tf_op jit(solution)/shard_map/all_to_all | solution.py:497
  123.7 0.0 copy-done.1
  123.7 1.1 copy.38
  124.8 15.7 %all-to-all-done.3 = bf16[16,32,1152]{2,1,0:T(8,128)(2,1)S(1)} async-done(((bf16[16,32,1152]{2,1,0:T(8,128)(2,1)}), bf16[16,32,1152]{2,1,0:T(8,128)(2,1)S(1)}, u32[]{:S(2)}, u32[]{:S(2)}) %all-to-all-start.3) | async-done | bytes 1179680 | tf_op jit(solution)/shard_map/all_to_all | solution.py:497
  140.5 4.1 %all-to-all-start.2 = ((bf16[16,32,1152]{2,1,0:T(8,128)(2,1)}), bf16[16,32,1152]{2,1,0:T(8,128)(2,1)S(1)}, u32[]{:S(2)}, u32[]{:S(2)}) async-start(bf16[16,32,1152]{2,1,0:T(8,128)(2,1)} %bitcast.14), calls=%async_computation.2 | async-start | bytes 2359296 | tf_op jit(solution)/shard_map/all_to_all | solution.py:497
  144.6 52.4 %shard_map.166 = (bf16[9,3456]{1,0:T(8,128)(2,1)}, bf16[9,1152]{1,0:T(8,128)(2,1)}) custom-call(bf16[4,1152,1152]{2,1,0:T(8,128)(2,1)} %get-tuple-element.11.gw, bf16[192,144]{1,0:T(8,128)(2,1)} %constant.15.clone.pad2, bf16[64,48]{1,0:T(8,128)(2,1)} %constant.16.clone.pad3), custom_call_target="tpu_custom_call" | custom-call | flops 1000000000 | bytes 20971520 | tf_op jit(solution)/shard_map/pallas_call | solution.py:214
  197.1 1.1 copy.41
  198.2 0.0 all-to-all-done.2
  198.2 0.0 copy-start.2
  198.2 0.0 copy-start.3
  198.2 1.1 copy.39
  199.3 0.0 copy-done.2
  199.3 0.6 copy.48
  199.9 0.0 copy-done.3
  199.9 0.6 copy.49
  (3 shorter events, 0.0 us)
Async XLA Ops:
  4.1 8.3 %copy-start = (bf16[1,2,256,1152]{3,2,1,0:T(8,128)(2,1)S(1)}, bf16[1,2,256,1152]{3,2,1,0:T(8,128)(2,1)}, u32[]{:S(2)}) copy-start(bf16[1,2,256,1152]{3,2,1,0:T(8,128)(2,1)} %param.22) | copy-start | bytes 3538948
  4.1 25.5 %all-to-all-start = ((bf16[2,256,1152]{2,0,1:T(2,128)(2,1)}), bf16[2,256,1152]{2,0,1:T(2,128)(2,1)S(1)}, u32[]{:S(2)}, u32[]{:S(2)}) async-start(bf16[2,256,1152]{2,0,1:T(2,128)(2,1)} %bitcast.35), calls=%async_computation | async-start | bytes 2359296 | tf_op jit(solution)/shard_map/all_to_all | solution.py:490
  29.7 4.6 %copy-start.5 = (f32[72]{0:T(128)S(1)}, f32[72]{0:T(128)}, u32[]{:S(2)}) copy-start(f32[72]{0:T(128)} %param.20) | copy-start | bytes 868
  29.7 5.3 %copy-start.4 = (f32[72]{0:T(128)S(1)}, f32[72]{0:T(128)}, u32[]{:S(2)}) copy-start(f32[72]{0:T(128)} %param.21) | copy-start | bytes 868
  29.7 21.4 %all-to-all-start.1 = ((bf16[2,256,1152]{2,0,1:T(2,128)(2,1)}), bf16[2,256,1152]{2,0,1:T(2,128)(2,1)S(1)}, u32[]{:S(2)}, u32[]{:S(2)}) async-start(bf16[2,256,1152]{2,0,1:T(2,128)(2,1)} %bitcast.34), calls=%async_computation.1 | async-start | bytes 2359296 | tf_op jit(solution)/shard_map/all_to_all | solution.py:490
  119.5 4.2 %copy-start.1 = (bf16[512,1152]{1,0:T(8,128)(2,1)S(1)}, bf16[512,1152]{1,0:T(8,128)(2,1)}, u32[]{:S(2)}) copy-start(bf16[512,1152]{1,0:T(8,128)(2,1)} %get-tuple-element.9) | copy-start | bytes 3538948
  119.5 21.0 %all-to-all-start.3 = ((bf16[16,32,1152]{2,1,0:T(8,128)(2,1)}), bf16[16,32,1152]{2,1,0:T(8,128)(2,1)S(1)}, u32[]{:S(2)}, u32[]{:S(2)}) async-start(bf16[16,32,1152]{2,1,0:T(8,128)(2,1)} %bitcast.20), calls=%async_computation.3 | async-start | bytes 2359296 | tf_op jit(solution)/shard_map/all_to_all | solution.py:497
  140.5 57.6 %all-to-all-start.2 = ((bf16[16,32,1152]{2,1,0:T(8,128)(2,1)}), bf16[16,32,1152]{2,1,0:T(8,128)(2,1)S(1)}, u32[]{:S(2)}, u32[]{:S(2)}) async-start(bf16[16,32,1152]{2,1,0:T(8,128)(2,1)} %bitcast.14), calls=%async_computation.2 | async-start | bytes 2359296 | tf_op jit(solution)/shard_map/all_to_all | solution.py:497
  198.2 1.1 copy-start.2
  198.2 1.8 copy-start.3

commit v3 on v2

--- a/solution.py
+++ b/solution.py
@@ -157,72 +157,6 @@
     ]
 
 
-def partners(xyz, core):
-    out = [device(shifted(xyz, d, k), core) for d in range(3) for k in (1, 2, 3)]
-    out.append(device(xyz, 1 - core))
-    return out
-
-
-def entry_barrier(devices):
-    sem = pltpu.get_barrier_semaphore()
-    for dev in devices:
-        pl.semaphore_signal(sem, inc=1, device_id=dev, device_id_type=MESH)
-    pl.semaphore_wait(sem, len(devices))
-
-
-def rs_kernel(gw, pad2, pad3, outq, outo, pair, psend, precv, *scratch):
-    xyz, core = coords()
-    entry_barrier(partners(xyz, core))
-    g = scratch[0]
-    pairs = []
-    for p in range(PARTS):
-        other = pl.ds(pl.multiple_of((1 - core) * 576, 576), 576)
-        c = pltpu.make_async_remote_copy(
-            src_ref=gw.at[p, other], dst_ref=pair.at[p], send_sem=psend.at[p], recv_sem=precv.at[p],
-            device_id=device(xyz, 1 - core), device_id_type=MESH)
-        c.start()
-        pairs.append(c)
-    parts = [Reduce(p, xyz, core, *scratch) for p in range(PARTS)]
-    for p in range(PARTS):
-        pairs[p].wait_recv()
-
-        def add(i, c, p=p):
-            r = pl.ds(pl.multiple_of(i * 16, 16), 16)
-            mine = pl.ds(pl.multiple_of(core * 576 + i * 16, 16), 16)
-            g[p, r] = (gw[p, mine].astype(F32) + pair[p, r].astype(F32)).astype(BF16)
-            return c
-
-        lax.fori_loop(0, 36, add, 0)
-        parts[p].start()
-    for r in parts:
-        r.forward()
-    for r in parts:
-        r.second(pad2)
-    for r in parts:
-        r.third(pad3)
-    for p in range(3):
-        outq[:, p * D:(p + 1) * D] = parts[p].finish()
-    outo[...] = parts[3].finish()
-    for c in pairs:
-        c.wait_send()
-
-
-def reduce_scatter(gw):
-    vm = pl.BlockSpec(memory_space=pltpu.VMEM)
-    pad2 = jnp.asarray(spread(36, 48), BF16)
-    pad3 = jnp.asarray(np.pad(spread(9, 16), ((0, 0), (0, 12))), BF16)
-    return pl.pallas_call(
-        rs_kernel,
-        out_shape=(jax.ShapeDtypeStruct((9, 3 * D), BF16), jax.ShapeDtypeStruct((9, D), BF16)),
-        in_specs=[vm] * 3,
-        out_specs=(vm, vm),
-        scratch_shapes=[pltpu.VMEM((PARTS, 576, D), BF16), pltpu.SemaphoreType.DMA((PARTS,)),
-                        pltpu.SemaphoreType.DMA((PARTS,))] + reduce_scratch(),
-        compiler_params=pltpu.CompilerParams(collective_id=0, has_side_effects=True, vmem_limit_bytes=56 * 1024 * 1024),
-        cost_estimate=pl.CostEstimate(flops=10**9, bytes_accessed=20 * 2**20, transcendentals=0),
-    )(gw, pad2, pad3)
-
-
 HD = 72
 NH = 16
 GR = 256
@@ -248,12 +182,21 @@
 
 
 LN_CH = 64
+FCH = LN_CH // 16
+
+
+def frames(i):
+    return pl.ds(i * FCH, FCH)
+
+
+def frame_rows(ref, g, i):
+    return ref[g, frames(i)].reshape(LN_CH, D)
 
 
 def ln_forward(g, tok, shift, scale, xh, rstd, hid):
     def body(i, c):
         r = sub_rows(g, i, LN_CH)
-        x = tok[r, :].astype(F32)
+        x = frame_rows(tok, g, i).astype(F32)
         xc = x - jnp.mean(x, axis=-1, keepdims=True)
         rs = lax.rsqrt(jnp.mean(xc * xc, axis=-1, keepdims=True) + 1e-6)
         n = xc * rs
@@ -273,7 +216,7 @@
         m1 = jnp.mean(gm, axis=-1, keepdims=True)
         m2 = jnp.mean(gm * n, axis=-1, keepdims=True)
         gx = rstd[r, :1] * (gm - m1 - n * m2)
-        gtok[r, :] = (cot[r, :].astype(F32) + gx).astype(BF16)
+        gtok[g, frames(i)] = (frame_rows(cot, g, i).astype(F32) + gx).astype(BF16).reshape(FCH, 16, D)
         return c
 
     lax.fori_loop(0, GR // LN_CH, body, 0, unroll=2)
@@ -383,66 +326,211 @@
 
 def out_projection(g, tok, att, wo, gate, out):
     r = group_rows(g)
-    out[r, :] = (tok[r, :].astype(F32) + gate[...] * dot_nn(att[r, :], wo[...])).astype(BF16)
+    y = tok[g].reshape(GR, D).astype(F32) + gate[...] * dot_nn(att[r, :], wo[...])
+    out[g] = y.astype(BF16).reshape(16, 16, D)
 
 
 def grad_att(g, cot, gate, wo, gp, gatt):
     r = group_rows(g)
-    x = (cot[r, :].astype(F32) * gate[...]).astype(BF16)
+    x = (cot[g].reshape(GR, D).astype(F32) * gate[...]).astype(BF16)
     gp[r, :] = x
     gatt[r, :] = dot_nt(x, wo[...]).astype(BF16)
 
 
-PCH = 192
-
-
 def permuted_t(p, x, idx, xt):
     def body(i, c):
-        r = pl.ds(pl.multiple_of(i * PCH, PCH), PCH)
-        lane = lax.broadcasted_iota(jnp.int32, (PCH, D), 1)
+        r = pl.ds(pl.multiple_of(i * 576, 64), 576)
+        lane = lax.broadcasted_iota(jnp.int32, (576, D), 1)
         m = jnp.where(idx[r, p:p + 1] == lane, 1.0, 0.0).astype(BF16)
-        xt[r, :] = dot_nt(m, x[...]).astype(BF16)
-        return c
-
-    lax.fori_loop(0, D // PCH, body, 0)
-
-
-def solo_kernel(tok, cot, shift, scale, gate, wqkv, wo, qg, kg, idx, ones_in, ones_out, out, gtok, gw,
-                hid, xh, rstd, proj, qn, kn, att, prob, gp, gatt, xt):
-    for g in range(2):
+        xt[p, r, :] = dot_nt(m, x[...]).astype(BF16)
+        return c
+
+    lax.fori_loop(0, 2, body, 0)
+
+
+class Exchange:
+    def __init__(self, a, send, recv, local, seq, dp):
+        self.a, self.send, self.recv, self.local, self.seq, self.dp = a, send, recv, local, seq, dp
+
+    def refs(self, g, peer):
+        raise NotImplementedError
+
+    def remote(self, g, k):
+        peer = lax.rem(self.seq + k, 8)
+        src, dst = self.refs(g, peer)
+        return pltpu.make_async_remote_copy(
+            src_ref=src, dst_ref=dst, send_sem=self.send.at[self.a, g, k], recv_sem=self.recv.at[self.a, g, k],
+            device_id=(self.dp, peer), device_id_type=MESH)
+
+    def own(self, g):
+        src, dst = self.refs(g, self.seq)
+        return pltpu.make_async_copy(src, dst, self.local.at[self.a, g])
+
+    def start(self, g):
+        for k in (1, 2, 3, 4, 5, 6, 7):
+            self.remote(g, k).start()
+        self.own(g).start()
+
+    def arrive(self, g):
+        for k in (1, 2, 3, 4, 5, 6, 7):
+            self.remote(g, k).wait_recv()
+        self.own(g).wait()
+
+    def leave(self, g):
+        for k in (1, 2, 3, 4, 5, 6, 7):
+            self.remote(g, k).wait_send()
+
+
+class Inward(Exchange):
+    def __init__(self, src, dst, *rest):
+        super().__init__(*rest)
+        self.src, self.dst = src, dst
+
+    def refs(self, g, peer):
+        rows = pl.ds(pl.multiple_of(peer * 32 + g * 16, 16), 16)
+        return self.src.at[0, :, rows, :], self.dst.at[g, pl.ds(self.seq * 2, 2)]
+
+
+class Outward(Inward):
+    def refs(self, g, peer):
+        rows = pl.ds(pl.multiple_of(self.seq * 32 + g * 16, 16), 16)
+        return self.src.at[g, pl.ds(peer * 2, 2)], self.dst.at[0, :, rows, :]
+
+
+def partners(xyz, core):
+    out = [device(shifted(xyz, d, k), core) for d in range(3) for k in (1, 2, 3)]
+    out.append(device(xyz, 1 - core))
+    far = shifted(xyz, 2, 2)
+    out.extend(device(shifted(far, 0, k), core) for k in (1, 2, 3))
+    return out
+
+
+def entry_barrier(devices):
+    sem = pltpu.get_barrier_semaphore()
+    for dev in devices:
+        pl.semaphore_signal(sem, inc=1, device_id=dev, device_id_type=MESH)
+    pl.semaphore_wait(sem, len(devices))
+
+
+def half(core):
+    return pl.ds(pl.multiple_of(core * 576, 64), 576)
+
+
+def kernel(tok_h, cot_h, wqkv_h, wo_h, shift, scale, gate, qg, kg, idx, ones_in, ones_out, pad2, pad3,
+           out_h, gtok_h, outq, outo,
+           tok, cot, wqkv, wo, hid, xh, rstd, proj, qn, kn, att, prob, gp, gatt, xt, out,
+           pout, pin, wsem, isend, irecv, ilocal, osend, orecv, olocal, psend, precv, *scratch):
+    g_ref = scratch[0]
+    cw = pltpu.make_async_copy(wqkv_h, wqkv, wsem.at[0])
+    co = pltpu.make_async_copy(wo_h, wo, wsem.at[1])
+    cw.start()
+    co.start()
+    xyz, core = coords()
+    dp, sq = lax.axis_index("dp"), lax.axis_index("seq")
+    entry_barrier(partners(xyz, core))
+    tok_in = Inward(tok_h, tok, 0, isend, irecv, ilocal, sq, dp)
+    cot_in = Inward(cot_h, cot, 1, isend, irecv, ilocal, sq, dp)
+    block_out = Outward(out, out_h, 0, osend, orecv, olocal, sq, dp)
+    gtok_out = Outward(tok, gtok_h, 1, osend, orecv, olocal, sq, dp)
+    for x in (tok_in, cot_in):
+        for g in range(2):
+            x.start(g)
+    parts = [Reduce(p, xyz, core, *scratch) for p in range(PARTS)]
+    cw.wait()
+    co.wait()
+
+    def forward(g, c):
+        tok_in.arrive(g)
         ln_forward(g, tok, shift, scale, xh, rstd, hid)
         r = group_rows(g)
-    for b in range(3):
-        cs = pl.ds(b * D, D)
-        proj[:, cs] = dot_nn(hid[...], wqkv[:, cs]).astype(BF16)
-    for g in range(2):
+        for b in range(3):
+            cs = pl.ds(b * D, D)
+            proj[r, cs] = dot_nn(hid[r, :], wqkv[:, cs]).astype(BF16)
         norm_forward(g, proj, qg, kg, qn, kn, ones_in, ones_out)
-
-    def fwd(g, c):
         att_forward(g, proj, qn, kn, att, prob)
-        return c
-
-    lax.fori_loop(0, 2, fwd, 0)
-    for g in range(2):
         out_projection(g, tok, att, wo, gate, out)
+        block_out.start(g)
+        return c
+
+    lax.fori_loop(0, 2, forward, 0)
+    permuted_t(3, att, idx, xt)
+    for p in range(3):
+        permuted_t(p, hid, idx, xt)
+
+    def gradient(g, c):
+        cot_in.arrive(g)
         grad_att(g, cot, gate, wo, gp, gatt)
-
-    permuted_t(3, att, idx, xt)
-    gw[3] = dot_nn(xt[...], gp[...]).astype(BF16)
-
-    def bwd(g, c):
+        return c
+
+    lax.fori_loop(0, 2, gradient, 0)
+
+    def pair(p):
+        return pltpu.make_async_remote_copy(
+            src_ref=pout.at[p % 3], dst_ref=pin.at[p], send_sem=psend.at[p], recv_sem=precv.at[p],
+            device_id=device(xyz, 1 - core), device_id_type=MESH)
+
+    def weight(p, right):
+        pout[p % 3] = dot_nn(xt[p, half(1 - core), :], right[...]).astype(BF16)
+        pair(p).start()
+        g_ref[p] = dot_nn(xt[p, half(core), :], right[...]).astype(BF16)
+
+    def reduce(p):
+        pair(p).wait_recv()
+
+        def add(i, c):
+            r = pl.ds(pl.multiple_of(i * 48, 16), 48)
+            g_ref[p, r] = (g_ref[p, r].astype(F32) + pin[p, r].astype(F32)).astype(BF16)
+            return c
+
+        lax.fori_loop(0, 12, add, 0)
+        parts[p].start()
+
+    weight(3, gp)
+    pair(3).wait_send()
+    reduce(3)
+
+    def backward(g, c):
         att_backward(g, proj, qn, kn, att, gatt, prob, ones_in)
-        return c
-
-    lax.fori_loop(0, 2, bwd, 0)
-    for g in range(2):
         norm_backward(g, proj, qg, kg, qn, kn, ones_in, ones_out)
-    for b in range(3):
-        permuted_t(b, hid, idx, xt)
-        gw[b] = dot_nn(xt[...], proj[:, pl.ds(b * D, D)]).astype(BF16)
-    gatt[...] = dot_nt(proj[...], wqkv[...]).astype(BF16)
-    for g in range(2):
-        ln_backward(g, gatt, cot, scale, xh, rstd, gtok)
+        return c
+
+    lax.fori_loop(0, 2, backward, 0)
+    parts[3].forward()
+    weight(2, proj.at[:, pl.ds(2 * D, D)])
+    weight(0, proj.at[:, pl.ds(0, D)])
+    reduce(2)
+    weight(1, proj.at[:, pl.ds(D, D)])
+    reduce(0)
+    parts[3].second(pad2)
+    reduce(1)
+
+    def leave(g, c):
+        r = group_rows(g)
+        gatt[r, :] = dot_nt(proj[r, :], wqkv[...]).astype(BF16)
+        ln_backward(g, gatt, cot, scale, xh, rstd, tok)
+        gtok_out.start(g)
+        return c
+
+    lax.fori_loop(0, 2, leave, 0)
+    for p in (2, 0, 1):
+        parts[p].forward()
+    parts[3].third(pad3)
+    for p in (2, 0, 1):
+        parts[p].second(pad2)
+    outo[...] = parts[3].finish()
+    for p in (2, 0, 1):
+        parts[p].third(pad3)
+    for p in (2, 0, 1):
+        outq[:, p * D:(p + 1) * D] = parts[p].finish()
+    for p in range(3):
+        pair(p).wait_send()
+    for x in (tok_in, cot_in):
+        for g in range(2):
+            x.leave(g)
+    for x in (block_out, gtok_out):
+        for g in range(2):
+            x.arrive(g)
+            x.leave(g)
 
 
 def ones_matrices():
@@ -451,24 +539,33 @@
     for h in range(NH):
         a[h * HD:(h + 1) * HD, h] = 1.0
         b[h, h * HD:(h + 1) * HD] = 1.0
-    return a, b
-
-
-def compute(tok, cot, shift, scale, gate, wqkv, wo, qg, kg):
+    return jnp.asarray(a, BF16), jnp.asarray(b, BF16)
+
+
+def on_device(tokens, mod_shift, mod_scale, res_gate, qkv_weight, out_weight, query_gain, key_gain, cotangent):
     vm = pl.BlockSpec(memory_space=pltpu.VMEM)
-    a, b = ones_matrices()
-    qgf = jnp.tile(qg * HD ** -0.5, (1, NH))
-    kgf = jnp.tile(kg, (1, NH))
+    anywhere = pl.BlockSpec(memory_space=pl.ANY)
+    ones_in, ones_out = ones_matrices()
+    pad2 = jnp.asarray(spread(36, 48), BF16)
+    pad3 = jnp.asarray(np.pad(spread(9, 16), ((0, 0), (0, 12))), BF16)
+    qg = jnp.tile(query_gain[None] * HD ** -0.5, (1, NH))
+    kg = jnp.tile(key_gain[None], (1, NH))
+    dma = pltpu.SemaphoreType.DMA
     return pl.pallas_call(
-        solo_kernel,
+        kernel,
         out_shape=(
-            jax.ShapeDtypeStruct((N, D), BF16),
-            jax.ShapeDtypeStruct((N, D), BF16),
-            jax.ShapeDtypeStruct((4, D, D), BF16),
+            jax.ShapeDtypeStruct(tokens.shape, BF16),
+            jax.ShapeDtypeStruct(tokens.shape, BF16),
+            jax.ShapeDtypeStruct((9, 3 * D), BF16),
+            jax.ShapeDtypeStruct((9, D), BF16),
         ),
-        in_specs=[vm] * 12,
-        out_specs=(vm,) * 3,
+        in_specs=[anywhere] * 4 + [vm] * 10,
+        out_specs=(anywhere, anywhere, vm, vm),
         scratch_shapes=[
+            pltpu.VMEM((2, 16, 16, D), BF16),
+            pltpu.VMEM((2, 16, 16, D), BF16),
+            pltpu.VMEM((D, 3 * D), BF16),
+            pltpu.VMEM((D, D), BF16),
             pltpu.VMEM((N, D), BF16),
             pltpu.VMEM((N, D), F32),
             pltpu.VMEM((N, 128), F32),
@@ -479,34 +576,20 @@
             pltpu.VMEM((2, NH, GR, GR), BF16),
             pltpu.VMEM((N, D), BF16),
             pltpu.VMEM((N, D), BF16),
-            pltpu.VMEM((D, N), BF16),
-        ],
-        compiler_params=pltpu.CompilerParams(vmem_limit_bytes=62 * 1024 * 1024),
-    )(tok, cot, shift, scale, gate, wqkv, wo, qgf, kgf, jnp.asarray(natural_rows()),
-      jnp.asarray(a, BF16), jnp.asarray(b, BF16))
-
-
-def to_groups(x):
-    y = lax.all_to_all(x[0], "seq", split_axis=1, concat_axis=0, tiled=True)
-    f, p, d = y.shape
-    return y.reshape(f, p // 16, 16, d).transpose(1, 0, 2, 3).reshape(f * p, d)
-
-
-def from_groups(y, frames, pos):
-    z = y.reshape(pos // 16, frames, 16, D).transpose(1, 0, 2, 3).reshape(frames, pos, D)
-    return lax.all_to_all(z, "seq", split_axis=0, concat_axis=1, tiled=True)[None]
-
-
-def on_device(tokens, mod_shift, mod_scale, res_gate, qkv_weight, out_weight, query_gain, key_gain, cotangent):
-    tok = to_groups(tokens)
-    cot = to_groups(cotangent)
-    n = tok.shape[0]
-    out, gtok, gw = compute(tok, cot, mod_shift, mod_scale, res_gate, qkv_weight, out_weight,
-                            query_gain[None], key_gain[None])
-    block_output = from_groups(out, 16, n // 16)
-    grad_tokens = from_groups(gtok, 16, n // 16)
-    grad_qkv_weight, grad_out_weight = reduce_scatter(gw)
-    return block_output, grad_tokens, grad_qkv_weight, grad_out_weight
+            pltpu.VMEM((PARTS, D, N), BF16),
+            pltpu.VMEM((2, 16, 16, D), BF16),
+            pltpu.VMEM((3, 576, D), BF16),
+            pltpu.VMEM((PARTS, 576, D), BF16),
+            dma((2,)),
+            dma((2, 2, 8)), dma((2, 2, 8)), dma((2, 2)),
+            dma((2, 2, 8)), dma((2, 2, 8)), dma((2, 2)),
+            dma((PARTS,)), dma((PARTS,)),
+        ] + reduce_scratch(),
+        compiler_params=pltpu.CompilerParams(collective_id=0, has_side_effects=True,
+                                             vmem_limit_bytes=63 * 1024 * 1024),
+        cost_estimate=pl.CostEstimate(flops=18 * 10**9, bytes_accessed=16 * 2**20, transcendentals=2**21),
+    )(tokens, cotangent, qkv_weight, out_weight, mod_shift, mod_scale, res_gate, qg, kg,
+      jnp.asarray(natural_rows()), ones_in, ones_out, pad2, pad3)
 
 
 def solution(mesh):

time: 204 us -> 121 us (0.59)
  the two profiles are of different devices: /device:TPU:1 before, /device:TPU:0 now
where the time goes in v3:
time: 121 us
  Pallas kernels  113 us (93%)
  local copies, waits for them, and re-layouts  6.79 us (6%)
    pallas_call x1, Pallas kernels, on_device(): pl.pallas_call(kernel, out_shape=(jax.ShapeDtypeStruct(tokens.shape, BF16...  113 us
    unnamed x10, local copies, waits for them, and re-layouts  4.75 us

profile of v3, /device:TPU:0, one launch (start us, length us, event | category | flops | bytes accessed | tf_op | source)
XLA Modules:
  0.0 120.6 jit_solution(12498619498003360520)
XLA Ops:
  0.6 0.7 broadcast_multiply_fusion
  1.3 0.7 tile.18.qg
  2.0 0.7 tile.19
  2.6 0.7 tile.20.kg
  3.3 112.5 %shard_map.165 = (bf16[1,2,256,1152]{3,2,1,0:T(8,128)(2,1)}, bf16[1,2,256,1152]{3,2,1,0:T(8,128)(2,1)}, bf16[9,3456]{1,0:T(8,128)(2,1)}, bf16[9,1152]{1,0:T(8,128)(2,1)}) custom-call(bf16[1,2,256,1152]{3,2,1,0:T(8,128)(2,1)} %tok_h.1, bf16[1,2,256,1152]{3,2,1,0:T(8,128)(2,1)} %cot_h.1, bf16[1152,3456]{1,0:T(8,128)(2,1)} %wqkv_h.1, bf16[1152,1152]{1,0:T(8,128)(2,1)} %wo_h.1, ...), custom_call_target="tpu_custom_call" | custom-call | flops 17999998976 | bytes 16777216 | tf_op jit(solution)/shard_map/pallas_call | solution.py:554
  115.9 0.0 copy-start
  115.9 2.5 %copy.22 = bf16[1,2,256,1152]{3,2,1,0:T(8,128)(2,1)} copy(bf16[1,2,256,1152]{3,2,1,0:T(8,128)(2,1)} %get-tuple-element.8) | data formatting | bytes 2359296
  118.3 0.0 copy-done
  118.3 0.0 copy-start.1
  118.3 0.0 copy-start.2
  118.3 1.0 copy.23
  119.4 0.0 copy-done.1
  119.4 0.6 copy.24
  120.0 0.0 copy-done.2
  120.0 0.6 copy.25
  (1 shorter events, 0.0 us)
Async XLA Ops:
  115.9 2.5 %copy-start = (bf16[1,2,256,1152]{3,2,1,0:T(8,128)(2,1)S(1)}, bf16[1,2,256,1152]{3,2,1,0:T(8,128)(2,1)}, u32[]{:S(2)}) copy-start(bf16[1,2,256,1152]{3,2,1,0:T(8,128)(2,1)} %get-tuple-element.9) | copy-start | bytes 3538948
  118.3 1.0 copy-start.1
  118.3 1.7 %copy-start.2 = (bf16[9,1152]{1,0:T(8,128)(2,1)S(1)}, bf16[9,1152]{1,0:T(8,128)(2,1)}, u32[]{:S(2)}) copy-start(bf16[9,1152]{1,0:T(8,128)(2,1)} %get-tuple-element.11) | copy-start | bytes 62212

commit v4 on v3

--- a/solution.py
+++ b/solution.py
@@ -210,16 +210,16 @@
 
 def ln_backward(g, gh, cot, scale, xh, rstd, gtok):
     def body(i, c):
-        r = sub_rows(g, i, LN_CH)
+        r = sub_rows(g, i, 16)
         n = xh[r, :]
         gm = gh[r, :].astype(F32) * (1.0 + scale[...])
         m1 = jnp.mean(gm, axis=-1, keepdims=True)
         m2 = jnp.mean(gm * n, axis=-1, keepdims=True)
         gx = rstd[r, :1] * (gm - m1 - n * m2)
-        gtok[g, frames(i)] = (frame_rows(cot, g, i).astype(F32) + gx).astype(BF16).reshape(FCH, 16, D)
-        return c
-
-    lax.fori_loop(0, GR // LN_CH, body, 0, unroll=2)
+        gtok[g, i] = (cot[g, i].astype(F32) + gx).astype(BF16)
+        return c
+
+    lax.fori_loop(0, 16, body, 0, unroll=4)
 
 
 def head_sum(x, ones_in):
@@ -416,15 +416,18 @@
     return pl.ds(pl.multiple_of(core * 576, 64), 576)
 
 
-def kernel(tok_h, cot_h, wqkv_h, wo_h, shift, scale, gate, qg, kg, idx, ones_in, ones_out, pad2, pad3,
+def kernel(tok_h, cot_h, wqkv_h, wo_h, shift, scale, gate, qg_h, kg_h, idx, ones_in, ones_out, pad2, pad3,
            out_h, gtok_h, outq, outo,
            tok, cot, wqkv, wo, hid, xh, rstd, proj, qn, kn, att, prob, gp, gatt, xt, out,
-           pout, pin, wsem, isend, irecv, ilocal, osend, orecv, olocal, psend, precv, *scratch):
+           pout, pin, wsem, qg, kg, isend, irecv, ilocal, osend, orecv, olocal, psend, precv, *scratch):
     g_ref = scratch[0]
     cw = pltpu.make_async_copy(wqkv_h, wqkv, wsem.at[0])
     co = pltpu.make_async_copy(wo_h, wo, wsem.at[1])
     cw.start()
     co.start()
+    for h in range(NH):
+        qg[:, pl.ds(h * HD, HD)] = qg_h[...] * HD ** -0.5
+        kg[:, pl.ds(h * HD, HD)] = kg_h[...]
     xyz, core = coords()
     dp, sq = lax.axis_index("dp"), lax.axis_index("seq")
     entry_barrier(partners(xyz, core))
@@ -548,8 +551,6 @@
     ones_in, ones_out = ones_matrices()
     pad2 = jnp.asarray(spread(36, 48), BF16)
     pad3 = jnp.asarray(np.pad(spread(9, 16), ((0, 0), (0, 12))), BF16)
-    qg = jnp.tile(query_gain[None] * HD ** -0.5, (1, NH))
-    kg = jnp.tile(key_gain[None], (1, NH))
     dma = pltpu.SemaphoreType.DMA
     return pl.pallas_call(
         kernel,
@@ -581,6 +582,7 @@
             pltpu.VMEM((3, 576, D), BF16),
             pltpu.VMEM((PARTS, 576, D), BF16),
             dma((2,)),
+            pltpu.VMEM((1, D), F32), pltpu.VMEM((1, D), F32),
             dma((2, 2, 8)), dma((2, 2, 8)), dma((2, 2)),
             dma((2, 2, 8)), dma((2, 2, 8)), dma((2, 2)),
             dma((PARTS,)), dma((PARTS,)),
@@ -588,7 +590,7 @@
         compiler_params=pltpu.CompilerParams(collective_id=0, has_side_effects=True,
                                              vmem_limit_bytes=63 * 1024 * 1024),
         cost_estimate=pl.CostEstimate(flops=18 * 10**9, bytes_accessed=16 * 2**20, transcendentals=2**21),
-    )(tokens, cotangent, qkv_weight, out_weight, mod_shift, mod_scale, res_gate, qg, kg,
+    )(tokens, cotangent, qkv_weight, out_weight, mod_shift, mod_scale, res_gate, query_gain[None], key_gain[None],
       jnp.asarray(natural_rows()), ones_in, ones_out, pad2, pad3)
 
 

time: 121 us -> 118 us (0.975)
  local copies, waits for them, and re-layouts: 6.79 us -> 4.75 us
    another operation x4 -> x0, local copies, waits for them, and re-layouts: 2.03 us -> none  [the longest x2 1.34 us: on_device(): kg = jnp.tile(key_gain[None], (1, NH))]
where the time goes in v4:
time: 118 us; the launch traced here: 117 us
  Pallas kernels  112 us (95%)
  local copies, waits for them, and re-layouts  4.75 us (4%)
    pallas_call x1, Pallas kernels, on_device(): pl.pallas_call(kernel, out_shape=(jax.ShapeDtypeStruct(tokens.shape, BF16...  112 us
    unnamed x10, local copies, waits for them, and re-layouts  4.75 us

profile of v4, /device:TPU:0, one launch (start us, length us, event | category | flops | bytes accessed | tf_op | source)
XLA Modules:
  0.0 117.5 jit_solution(14969327744240614859)
XLA Ops:
  0.6 112.0 %shard_map.165 = (bf16[1,2,256,1152]{3,2,1,0:T(8,128)(2,1)}, bf16[1,2,256,1152]{3,2,1,0:T(8,128)(2,1)}, bf16[9,3456]{1,0:T(8,128)(2,1)}, bf16[9,1152]{1,0:T(8,128)(2,1)}) custom-call(bf16[1,2,256,1152]{3,2,1,0:T(8,128)(2,1)} %tok_h.1, bf16[1,2,256,1152]{3,2,1,0:T(8,128)(2,1)} %cot_h.1, bf16[1152,3456]{1,0:T(8,128)(2,1)} %wqkv_h.1, bf16[1152,1152]{1,0:T(8,128)(2,1)} %wo_h.1, ...), custom_call_target="tpu_custom_call" | custom-call | flops 17999998976 | bytes 16777216 | tf_op jit(solution)/shard_map/pallas_call | solution.py:555
  112.7 0.0 copy-start
  112.7 2.5 %copy.22 = bf16[1,2,256,1152]{3,2,1,0:T(8,128)(2,1)} copy(bf16[1,2,256,1152]{3,2,1,0:T(8,128)(2,1)} %get-tuple-element.8) | data formatting | bytes 2359296
  115.2 0.0 copy-done
  115.2 0.0 copy-start.1
  115.2 0.0 copy-start.2
  115.2 1.0 copy.23
  116.2 0.0 copy-done.1
  116.2 0.6 copy.24
  116.8 0.0 copy-done.2
  116.8 0.6 copy.25
Async XLA Ops:
  112.7 2.5 %copy-start = (bf16[1,2,256,1152]{3,2,1,0:T(8,128)(2,1)S(1)}, bf16[1,2,256,1152]{3,2,1,0:T(8,128)(2,1)}, u32[]{:S(2)}) copy-start(bf16[1,2,256,1152]{3,2,1,0:T(8,128)(2,1)} %get-tuple-element.9) | copy-start | bytes 3538948
  115.2 1.0 copy-start.1
  115.2 1.7 %copy-start.2 = (bf16[9,1152]{1,0:T(8,128)(2,1)S(1)}, bf16[9,1152]{1,0:T(8,128)(2,1)}, u32[]{:S(2)}) copy-start(bf16[9,1152]{1,0:T(8,128)(2,1)} %get-tuple-element.11) | copy-start | bytes 62212

commit v5 on v4

--- a/solution.py
+++ b/solution.py
@@ -229,7 +229,7 @@
 def head_spread(m, ones_out):
     hi = m.astype(BF16)
     lo = (m - hi.astype(F32)).astype(BF16)
-    return dot_nn(hi, ones_out[...]) + dot_nn(lo, ones_out[...])
+    return dot_nn(jnp.concatenate([hi, lo], axis=1), ones_out[...])
 
 
 def norm_forward(g, proj, qg, kg, qn, kn, ones_in, ones_out):
@@ -500,30 +500,31 @@
     lax.fori_loop(0, 2, backward, 0)
     parts[3].forward()
     weight(2, proj.at[:, pl.ds(2 * D, D)])
+    weight(1, proj.at[:, pl.ds(D, D)])
+    reduce(2)
     weight(0, proj.at[:, pl.ds(0, D)])
-    reduce(2)
-    weight(1, proj.at[:, pl.ds(D, D)])
+    reduce(1)
+    parts[3].second(pad2)
     reduce(0)
-    parts[3].second(pad2)
-    reduce(1)
-
-    def leave(g, c):
+
+    def leave(g):
         r = group_rows(g)
         gatt[r, :] = dot_nt(proj[r, :], wqkv[...]).astype(BF16)
         ln_backward(g, gatt, cot, scale, xh, rstd, tok)
         gtok_out.start(g)
-        return c
-
-    lax.fori_loop(0, 2, leave, 0)
-    for p in (2, 0, 1):
-        parts[p].forward()
+
+    leave(0)
+    parts[2].forward()
+    parts[1].forward()
+    leave(1)
+    parts[0].forward()
     parts[3].third(pad3)
-    for p in (2, 0, 1):
+    for p in (2, 1, 0):
         parts[p].second(pad2)
     outo[...] = parts[3].finish()
-    for p in (2, 0, 1):
+    for p in (2, 1, 0):
         parts[p].third(pad3)
-    for p in (2, 0, 1):
+    for p in (2, 1, 0):
         outq[:, p * D:(p + 1) * D] = parts[p].finish()
     for p in range(3):
         pair(p).wait_send()
@@ -538,10 +539,11 @@
 
 def ones_matrices():
     a = np.zeros((D, 128), np.float32)
-    b = np.zeros((128, D), np.float32)
+    b = np.zeros((256, D), np.float32)
     for h in range(NH):
         a[h * HD:(h + 1) * HD, h] = 1.0
         b[h, h * HD:(h + 1) * HD] = 1.0
+        b[128 + h, h * HD:(h + 1) * HD] = 1.0
     return jnp.asarray(a, BF16), jnp.asarray(b, BF16)
 
 

time: 118 us -> 116 us (0.983)
    pallas_call x1, Pallas kernels: 112 us -> 111 us  [on_device(): pl.pallas_call(kernel, out_shape=(jax.ShapeDtypeStruct(tokens.shape, BF16...]
where the time goes in v5:
time: 116 us
  Pallas kernels  111 us (96%)
  local copies, waits for them, and re-layouts  4.75 us (4%)
    pallas_call x1, Pallas kernels, on_device(): pl.pallas_call(kernel, out_shape=(jax.ShapeDtypeStruct(tokens.shape, BF16...  111 us
    unnamed x10, local copies, waits for them, and re-layouts  4.75 us

profile of v5, /device:TPU:0, one launch (start us, length us, event | category | flops | bytes accessed | tf_op | source)
XLA Modules:
  0.0 116.2 jit_solution(10559682159541847085)
XLA Ops:
  0.6 110.8 %shard_map.165 = (bf16[1,2,256,1152]{3,2,1,0:T(8,128)(2,1)}, bf16[1,2,256,1152]{3,2,1,0:T(8,128)(2,1)}, bf16[9,3456]{1,0:T(8,128)(2,1)}, bf16[9,1152]{1,0:T(8,128)(2,1)}) custom-call(bf16[1,2,256,1152]{3,2,1,0:T(8,128)(2,1)} %tok_h.1, bf16[1,2,256,1152]{3,2,1,0:T(8,128)(2,1)} %cot_h.1, bf16[1152,3456]{1,0:T(8,128)(2,1)} %wqkv_h.1, bf16[1152,1152]{1,0:T(8,128)(2,1)} %wo_h.1, ...), custom_call_target="tpu_custom_call" | custom-call | flops 17999998976 | bytes 16777216 | tf_op jit(solution)/shard_map/pallas_call | solution.py:557
  111.5 0.0 copy-start
  111.5 2.5 %copy.22 = bf16[1,2,256,1152]{3,2,1,0:T(8,128)(2,1)} copy(bf16[1,2,256,1152]{3,2,1,0:T(8,128)(2,1)} %get-tuple-element.8) | data formatting | bytes 2359296
  113.9 0.0 copy-done
  113.9 0.0 copy-start.1
  113.9 0.0 copy-start.2
  113.9 1.0 copy.23
  115.0 0.0 copy-done.1
  115.0 0.6 copy.24
  115.6 0.0 copy-done.2
  115.6 0.6 copy.25
Async XLA Ops:
  111.5 2.5 %copy-start = (bf16[1,2,256,1152]{3,2,1,0:T(8,128)(2,1)S(1)}, bf16[1,2,256,1152]{3,2,1,0:T(8,128)(2,1)}, u32[]{:S(2)}) copy-start(bf16[1,2,256,1152]{3,2,1,0:T(8,128)(2,1)} %get-tuple-element.9) | copy-start | bytes 3538948
  113.9 1.0 copy-start.1
  113.9 1.7 %copy-start.2 = (bf16[9,1152]{1,0:T(8,128)(2,1)S(1)}, bf16[9,1152]{1,0:T(8,128)(2,1)}, u32[]{:S(2)}) copy-start(bf16[9,1152]{1,0:T(8,128)(2,1)} %get-tuple-element.11) | copy-start | bytes 62212
